TPU v7x, 128 devices: a whole 4x4x4 slice. The times are simulated.
128 devices in a mesh: dp: 8 (over y_hi, x), ctx: 16 (over z, y_lo, core).
Axes of the slice: x: 4, y: 4 (y_hi: 2, y_lo: 2; y = y_hi * 2 + y_lo), z: 4, core: 2. Of those that a mesh axis runs over, the one named last changes fastest.
Arguments:
- patches: bfloat16 [16384, 1280], P(('dp', 'ctx')), may hold values from -45 to 45
- vision_gain: float32 [1280], replicated, may hold values from 0.25 to 1.75
- vision_bias: float32 [1280], replicated, may hold values from -1.75 to 1.75
- up_weight: bfloat16 [2560, 1280], P(('dp', 'ctx')), may hold values from -0.15625 to 0.15625
- down_weight: bfloat16 [2560, 1280], P(('dp', 'ctx')), may hold values from -0.125 to 0.125
- merge_gain: float32 [1280], replicated, may hold values from 0.25 to 1.75
- merge_bias: float32 [1280], replicated, may hold values from -1.75 to 1.75
- merge_weight: bfloat16 [5120, 8192], P(None, 'dp'), may hold values from -0.078125 to 0.078125
- attn_gain: float32 [8192], replicated, may hold values from 0.25 to 1.75
- query_weight: bfloat16 [8192, 4096], P(None, 'dp'), may hold values from -0.1875 to 0.1875
- kv_weight: bfloat16 [2, 8192, 1024], P(None, None, 'dp'), may hold values from -0.0625 to 0.0625
- text_query: bfloat16 [10240, 4096], P('ctx', 'dp'), may hold values from -120 to 120, as said below
- text_kv: bfloat16 [2, 10240, 1024], P(None, 'ctx', 'dp'), may hold values from -6 to 6, as said below
- doc_ids: int32 [10240], P('ctx'), may hold values from 0 to 3, never falling along the last dimension, each value on 1 to 5120 neighbouring positions
- image_sizes: int32 [128, 4], P(('dp', 'ctx')), may hold values from 1 to 16, as said below
- image_offsets: int32 [128, 4], P(('dp', 'ctx')), may hold values from 0 to 10239, as said below
Outputs:
- context: bfloat16 [10240, 4096], P('ctx', 'dp')
Inputs may be any that keep to these rules, and one draw needn't show every extreme that they name: `image_sizes`: the 4 images of one device hold 32 merged rows together, and one of them holds exactly 16. `image_offsets`: images never intersect; each lies within the 640 positions of one index of ctx; the images of one index of ctx (over all of dp) put at most 32 rows into the positions of one index of ctx, and in every draw some index of ctx takes exactly 32 rows from every index. `text_query`: rows at image positions are not read. `text_kv`: rows at image positions are not read.
All inputs are finite; a program needn't handle non-finite values.
Results may differ from a plain program's by a relative error of at most 0.035.
Values may be sent and summed in bfloat16 or wider, within the bound.
No kernel may reach another device: no remote copies, remote signals or barrier semaphores. Data moves between devices by JAX's collectives and lax.ppermute only.
A program may use at most 128 MiB of HBM per device.

v0:
```python
import math

import jax
import jax.numpy as jnp
import numpy as np
from jax import lax
from jax.experimental import pallas as pl
from jax.experimental.pallas import tpu as pltpu
from jax.sharding import Mesh
from jax.sharding import PartitionSpec as P

HEAD_DIM = 128
MOST = 16
SEQ = 640
REACH = 8
WINDOW = SEQ * (REACH + 1)
KEY_BLOCK = 640
PADDED = -(-WINDOW // KEY_BLOCK) * KEY_BLOCK
QUERY_BLOCK = 640
GROUP = 4
IMAGES = 512
PLACE_UNROLL = 4
CAPACITY = 32
CHUNK = 16
UNITS = 24
CTX_COUNT = 16
DP_COUNT = 8

MASKED_SCORE = -1e30
LOWEST_PEAK = -1e29
EPSILON = 1e-06
DP = ("yh", "x")
CTX = ("z", "yl", "c")


def layer_norm(rows_in, norm_gain, norm_bias):
    values = rows_in.astype(jnp.float32)
    center = values - jnp.mean(values, axis=-1, keepdims=True)
    spread = jnp.mean(center * center, axis=-1, keepdims=True)
    return (center * lax.rsqrt(spread + EPSILON) * norm_gain + norm_bias).astype(jnp.bfloat16)


def quick_gelu(values):
    return values * jax.nn.sigmoid(1.702 * values)


def starts_within(sizes):
    count = sizes.shape[-1]
    earlier = jnp.arange(count)[None, :] < jnp.arange(count)[:, None]
    return jnp.sum(jnp.where(earlier, sizes[..., None, :], 0), axis=-1, dtype=jnp.int32)


def row_positions(size_table, offset_table, row_count):
    image_starts = starts_within(size_table)
    image_ends = image_starts + size_table
    within = jnp.arange(row_count, dtype=jnp.int32)[None, :, None]
    inside = (within >= image_starts[:, None, :]) & (within < image_ends[:, None, :])
    placed = offset_table[:, None, :] - image_starts[:, None, :] + within
    return jnp.sum(jnp.where(inside, placed, 0), axis=2, dtype=jnp.int32)


def gather_by_exchange(block, axes, count):
    return lax.all_to_all(
        jnp.broadcast_to(block[None], (count,) + block.shape), axes, split_axis=0, concat_axis=0
    )


def swap(rows, axis):
    return lax.ppermute(rows, axis, [(0, 1), (1, 0)])


def attention_kernel(
    info,
    image_src,
    image_dst,
    image_len,
    blocks_at,
    text_query_ref,
    bring_ref,
    low_ref,
    first_near_ref,
    first_far_ref,
    last_ref,
    text_near_ref,
    text_far_ref,
    out_ref,
    text_held,
    key_wide,
    value_wide,
    image_key,
    image_value,
    image_query,
    key_held,
    value_held,
    sems,
):
    query_offset = info[1]
    half = CTX_COUNT // 2
    near = text_near_ref.shape[0]
    copies = []
    for shard in range(REACH + 1):
        at = blocks_at[CTX_COUNT + shard]
        target = text_held.at[pl.ds(shard * SEQ, SEQ), :]

        @pl.when(at < near)
        def _(at=at, target=target, shard=shard):
            pltpu.make_async_copy(text_near_ref.at[at], target, sems.at[shard]).start()

        @pl.when(at >= near)
        def _(at=at, target=target, shard=shard):
            pltpu.make_async_copy(text_far_ref.at[at - near], target, sems.at[shard]).start()

        copies.append(pltpu.make_async_copy(text_near_ref.at[0], target, sems.at[shard]))

    for side, first_ref in enumerate((first_near_ref, first_far_ref)):

        def widen_first(block, unused, side=side, first_ref=first_ref):
            source = blocks_at[side * half + block]
            for device in range(DP_COUNT):
                base = source * (DP_COUNT * CAPACITY) + device * CAPACITY
                rows = pl.ds(pl.multiple_of(base, CHUNK), CHUNK)
                held = first_ref[block, device * CHUNK : (device + 1) * CHUNK, :].astype(
                    jnp.float32
                )
                image_key[rows, :] = held[:, :HEAD_DIM]
                image_value[rows, :] = held[:, HEAD_DIM:]
            return unused

        lax.fori_loop(0, half, widen_first, 0)

    def widen_last(source, unused):
        for device in range(DP_COUNT):
            base = source * (DP_COUNT * CAPACITY) + device * CAPACITY + CHUNK
            rows = pl.ds(pl.multiple_of(base, CHUNK), CHUNK)
            at, side = device % 4 * CHUNK, device // 4 * 2 * HEAD_DIM
            held = last_ref[source, at : at + CHUNK, side : side + 2 * HEAD_DIM].astype(jnp.float32)
            image_key[rows, :] = held[:, :HEAD_DIM]
            image_value[rows, :] = held[:, HEAD_DIM:]
        rows = pl.ds(pl.multiple_of(source * CAPACITY, CAPACITY), CAPACITY)
        image_query[rows, :] = last_ref[source, 4 * CHUNK :, :]
        return unused

    lax.fori_loop(0, CTX_COUNT, widen_last, 0)
    for shard in range(REACH + 1):
        copies[shard].wait()

    def widen_text(step, unused):
        rows = pl.ds(pl.multiple_of(step * 320, 320), 320)
        key_wide[rows, :] = text_held[rows, :HEAD_DIM].astype(jnp.float32)
        value_wide[rows, :] = text_held[rows, HEAD_DIM:].astype(jnp.float32)
        return unused

    lax.fori_loop(0, WINDOW // 320, widen_text, 0)
    row_in = lax.broadcasted_iota(jnp.int32, (MOST, HEAD_DIM), 0)

    def place(step, unused):
        for lane in range(PLACE_UNROLL):
            image = step * PLACE_UNROLL + lane
            target = image_dst[image]
            origin = image_src[image]
            taken = row_in < image_len[image]
            rows = pl.ds(target, MOST)
            pltpu.store(key_wide.at[rows, :], image_key[pl.ds(origin, MOST), :], mask=taken)
            pltpu.store(value_wide.at[rows, :], image_value[pl.ds(origin, MOST), :], mask=taken)
        return unused

    lax.fori_loop(0, IMAGES // PLACE_UNROLL, place, 0)

    def narrow(step, unused):
        rows = pl.ds(pl.multiple_of(step * HEAD_DIM, HEAD_DIM), HEAD_DIM)
        key_held[rows, :] = key_wide[rows, :].astype(jnp.bfloat16)
        value_held[:HEAD_DIM, rows] = value_wide[rows, :].T.astype(jnp.bfloat16)
        return unused

    lax.fori_loop(0, WINDOW // HEAD_DIM, narrow, 0)
    value_held[HEAD_DIM:, :] = jnp.ones((CHUNK, PADDED), jnp.bfloat16)
    if PADDED > WINDOW:
        key_held[WINDOW:, :] = jnp.zeros((PADDED - WINDOW, HEAD_DIM), jnp.bfloat16)
        value_held[:HEAD_DIM, WINDOW:] = jnp.zeros((HEAD_DIM, PADDED - WINDOW), jnp.bfloat16)

    across = GROUP * QUERY_BLOCK
    to_power = math.log2(math.e) / math.sqrt(HEAD_DIM)
    column_at = lax.broadcasted_iota(jnp.int32, (1, QUERY_BLOCK), 1)

    def query_step(block, unused):
        rows = pl.ds(pl.multiple_of(block * QUERY_BLOCK, QUERY_BLOCK), QUERY_BLOCK)
        first = query_offset + block * QUERY_BLOCK
        bring = bring_ref[rows, :]
        is_image = jnp.max(bring.astype(jnp.float32), axis=-1, keepdims=True) > 0.5
        placed = jnp.where(
            is_image,
            jnp.dot(bring, image_query[...], preferred_element_type=jnp.float32),
            text_query_ref[rows, :].astype(jnp.float32),
        )
        queries = jnp.concatenate(
            [placed[:, h * HEAD_DIM : (h + 1) * HEAD_DIM].T for h in range(GROUP)], axis=1
        ).astype(jnp.bfloat16)
        lows = jnp.concatenate([low_ref[:, rows]] * GROUP, axis=1)
        highs = jnp.concatenate([column_at + first] * GROUP, axis=1)
        low_first = info[2 + 2 * block]
        low_last = info[3 + 2 * block]
        begin = low_first // KEY_BLOCK
        end = (first + QUERY_BLOCK - 1) // KEY_BLOCK + 1
        clear_begin = jnp.minimum((low_last + KEY_BLOCK - 1) // KEY_BLOCK, end)
        clear_end = jnp.maximum((first + 1) // KEY_BLOCK, clear_begin)

        def key_step(at, running, masked):
            peak, gathered = running
            keys_at = pl.ds(pl.multiple_of(at * KEY_BLOCK, KEY_BLOCK), KEY_BLOCK)
            scores = jnp.dot(key_held[keys_at, :], queries, preferred_element_type=jnp.float32)
            if masked:
                place_at = at * KEY_BLOCK + lax.broadcasted_iota(jnp.int32, (KEY_BLOCK, 1), 0)
                scores = jnp.where((place_at >= lows) & (place_at <= highs), scores, MASKED_SCORE)
            new_peak = jnp.maximum(peak, jnp.max(scores, axis=0, keepdims=True))
            weights = jnp.exp2((scores - new_peak) * to_power).astype(jnp.bfloat16)
            rescale = jnp.exp2((peak - new_peak) * to_power)
            gathered = gathered * rescale + jnp.dot(
                value_held[:, keys_at], weights, preferred_element_type=jnp.float32
            )
            return new_peak, gathered

        running = (
            jnp.full((1, across), LOWEST_PEAK, jnp.float32),
            jnp.zeros((HEAD_DIM + CHUNK, across), jnp.float32),
        )
        running = lax.fori_loop(begin, clear_begin, lambda a, r: key_step(a, r, True), running)
        running = lax.fori_loop(clear_begin, clear_end, lambda a, r: key_step(a, r, False), running)
        peak, gathered = lax.fori_loop(clear_end, end, lambda a, r: key_step(a, r, True), running)
        context = gathered[:HEAD_DIM] / gathered[HEAD_DIM : HEAD_DIM + 1]
        for h in range(GROUP):
            out_ref[rows, h * HEAD_DIM : (h + 1) * HEAD_DIM] = context[
                :, h * QUERY_BLOCK : (h + 1) * QUERY_BLOCK
            ].T.astype(jnp.bfloat16)
        return unused

    lax.fori_loop(0, SEQ // QUERY_BLOCK, query_step, 0)


def attention(tables, text_query, bring_in, low_rows, first, last, text):
    smem = pl.BlockSpec(memory_space=pltpu.SMEM)
    vmem = pl.BlockSpec(memory_space=pltpu.VMEM)
    image_rows = CTX_COUNT * DP_COUNT * CAPACITY
    return pl.pallas_call(
        attention_kernel,
        out_shape=jax.ShapeDtypeStruct(text_query.shape, jnp.bfloat16),
        in_specs=[smem] * 5 + [vmem] * 6 + [pl.BlockSpec(memory_space=pl.ANY)] * 2,
        out_specs=vmem,
        scratch_shapes=[
            pltpu.VMEM((WINDOW, 2 * HEAD_DIM), jnp.bfloat16),
            pltpu.VMEM((WINDOW + MOST, HEAD_DIM), jnp.float32),
            pltpu.VMEM((WINDOW + MOST, HEAD_DIM), jnp.float32),
            pltpu.VMEM((image_rows + MOST, HEAD_DIM), jnp.float32),
            pltpu.VMEM((image_rows + MOST, HEAD_DIM), jnp.float32),
            pltpu.VMEM((CTX_COUNT * CAPACITY, GROUP * HEAD_DIM), jnp.bfloat16),
            pltpu.VMEM((PADDED, HEAD_DIM), jnp.bfloat16),
            pltpu.VMEM((HEAD_DIM + CHUNK, PADDED), jnp.bfloat16),
            pltpu.SemaphoreType.DMA((REACH + 1,)),
        ],
        compiler_params=pltpu.CompilerParams(vmem_limit_bytes=48 * 1024 * 1024),
        cost_estimate=pl.CostEstimate(
            flops=8_000_000_000, bytes_accessed=8_000_000, transcendentals=13_000_000
        ),
    )(*tables, text_query, bring_in, low_rows, *first, last, *text)


def project_kernel(rows_ref, gain_ref, query_weight_ref, kv_weight_ref, query_ref, kv_ref, query_sum, kv_sum, squares):
    step = pl.program_id(0)

    @pl.when(step == 0)
    def _():
        query_sum[...] = jnp.zeros_like(query_sum)
        kv_sum[...] = jnp.zeros_like(kv_sum)
        squares[...] = jnp.zeros_like(squares)

    values = rows_ref[0].astype(jnp.float32)
    squares[...] += jnp.sum(values * values, axis=-1, keepdims=True)
    gained = (values * gain_ref[0]).astype(jnp.bfloat16)
    query_sum[...] += jnp.dot(gained, query_weight_ref[...], preferred_element_type=jnp.float32)
    kv_sum[:, :HEAD_DIM] += jnp.dot(gained, kv_weight_ref[0], preferred_element_type=jnp.float32)
    kv_sum[:, HEAD_DIM:] += jnp.dot(gained, kv_weight_ref[1], preferred_element_type=jnp.float32)

    @pl.when(step == DP_COUNT - 1)
    def _():
        scale = lax.rsqrt(squares[...] / (DP_COUNT * rows_ref.shape[2]) + EPSILON)
        query_ref[...] = (query_sum[...] * scale).astype(jnp.bfloat16)
        kv_ref[...] = (kv_sum[...] * scale).astype(jnp.bfloat16)


def project(whole, gain, query_weight, kv_weight):
    count, rows, part = whole.shape
    query_width, kv_width = query_weight.shape[1], kv_weight.shape[2]
    return pl.pallas_call(
        project_kernel,
        grid=(count,),
        out_shape=(
            jax.ShapeDtypeStruct((rows, query_width), jnp.bfloat16),
            jax.ShapeDtypeStruct((rows, 2 * kv_width), jnp.bfloat16),
        ),
        in_specs=[
            pl.BlockSpec((1, rows, part), lambda k: (k, 0, 0)),
            pl.BlockSpec((1, 1, part), lambda k: (k, 0, 0)),
            pl.BlockSpec((part, query_width), lambda k: (k, 0)),
            pl.BlockSpec((2, part, kv_width), lambda k: (0, k, 0)),
        ],
        out_specs=(
            pl.BlockSpec((rows, query_width), lambda k: (0, 0)),
            pl.BlockSpec((rows, 2 * kv_width), lambda k: (0, 0)),
        ),
        scratch_shapes=[
            pltpu.VMEM((rows, query_width), jnp.float32),
            pltpu.VMEM((rows, 2 * kv_width), jnp.float32),
            pltpu.VMEM((rows, 1), jnp.float32),
        ],
        compiler_params=pltpu.CompilerParams(vmem_limit_bytes=24 * 1024 * 1024),
        cost_estimate=pl.CostEstimate(
            flops=2 * rows * count * part * (query_width + 2 * kv_width),
            bytes_accessed=2 * count * part * (query_width + 2 * kv_width + rows),
            transcendentals=0,
        ),
    )(whole, gain, query_weight, kv_weight)


def body(
    patches,
    vision_gain,
    vision_bias,
    up_weight,
    down_weight,
    merge_gain,
    merge_bias,
    merge_weight,
    attn_gain,
    query_weight,
    kv_weight,
    text_query,
    text_kv,
    doc_ids,
    image_sizes,
    image_offsets,
):
    z_at, yl_at, c_at = lax.axis_index("z"), lax.axis_index("yl"), lax.axis_index("c")
    ctx_index = lax.axis_index(CTX)
    width = patches.shape[1]
    own_rows = patches.shape[0]
    units_own = up_weight.shape[0]

    below = jnp.sum(
        (doc_ids[:, None] < jnp.arange(4, dtype=jnp.int32)[None, :]).astype(jnp.int32),
        axis=0,
        dtype=jnp.int32,
    )
    facts = jnp.concatenate([image_sizes, image_offsets, below[None, :]], axis=1)
    facts = jnp.concatenate([facts // 128, facts % 128], axis=1).astype(jnp.bfloat16)
    fact_count = facts.shape[1]
    block = jnp.concatenate(
        [
            jnp.pad(up_weight, ((0, UNITS - units_own), (0, 0))),
            down_weight,
            jnp.pad(facts, ((0, UNITS - units_own - 1), (0, width - fact_count))),
        ],
        axis=0,
    )
    block = jnp.broadcast_to(block[None], (16,) + block.shape)
    block, patches = lax.optimization_barrier((block, patches))
    units = lax.all_to_all(block, DP + ("yl",), split_axis=0, concat_axis=0)
    normed = layer_norm(patches, vision_gain, vision_bias)
    column = jnp.concatenate(
        [normed]
        + [
            lax.ppermute(normed, "z", [(i, (i + step) % 4) for i in range(4)])
            for step in (1, 2, 3)
        ],
        axis=0,
    )
    near_rows = column.shape[0]
    near = jnp.concatenate([column, swap(column, "c")], axis=0)
    ups = units[:, :UNITS].reshape(-1, width)
    downs = units[:, UNITS:].reshape(-1, width)
    facts = units[:, UNITS + units_own, :fact_count].reshape(1, -1)
    hidden = quick_gelu(
        lax.dot_general(near, ups, (((1,), (1,)), ((), ())), preferred_element_type=jnp.float32)
    ).astype(jnp.bfloat16)
    away = jnp.dot(hidden[near_rows:], downs, preferred_element_type=jnp.float32).astype(
        jnp.bfloat16
    )
    here = jnp.dot(hidden[:near_rows], downs, preferred_element_type=jnp.float32)
    came = swap(
        jnp.concatenate(
            [away, jnp.pad(facts, ((0, CHUNK - 1), (0, width - facts.shape[1])))], axis=0
        ),
        "c",
    )
    pair_sum = (here + came[:near_rows].astype(jnp.float32)).astype(jnp.bfloat16)
    other = came[near_rows : near_rows + 1, : facts.shape[1]]
    facts = jnp.concatenate(
        [jnp.where(c_at == 0, facts, other), jnp.where(c_at == 0, other, facts)], axis=1
    )
    tail = jnp.pad(facts, ((0, CHUNK - 1), (0, width - facts.shape[1])))
    by_z = pair_sum.reshape(4, own_rows, width)
    terms = lax.all_to_all(
        jnp.stack(
            [
                jnp.concatenate(
                    [lax.dynamic_index_in_dim(by_z, (z_at - j + 4) % 4, 0, False), tail], axis=0
                )
                for j in range(4)
            ]
        ),
        "z",
        split_axis=0,
        concat_axis=0,
    )
    branch = jnp.sum(terms[:, :own_rows].astype(jnp.float32), axis=0)
    facts = terms[:, own_rows, : facts.shape[1]].astype(jnp.int32)
    facts = facts.reshape(4, 2, 8, 2, fact_count).transpose(2, 0, 3, 1, 4)
    facts = facts.reshape(8, 16, 2, fact_count // 2)
    facts = facts[:, :, 0] * 128 + facts[:, :, 1]
    vision = (patches.astype(jnp.float32) + branch).astype(jnp.bfloat16)
    merged_in = layer_norm(vision, merge_gain, merge_bias).reshape(-1, 4 * width)

    text = jnp.concatenate([text_kv[0], text_kv[1]], axis=1)
    text, merged_in = lax.optimization_barrier((text, merged_in))
    text = jnp.concatenate(
        [
            text,
            lax.ppermute(text, "z", [(0, 1), (1, 2), (2, 3)]),
            lax.ppermute(text, "z", [(0, 2), (1, 3)]),
        ],
        axis=0,
    )
    columns = [
        gather_by_exchange(merged_in[at : at + CHUNK], DP, DP_COUNT).reshape(-1, 4 * width)
        for at in (0, CHUNK)
    ]
    text, columns[0] = lax.optimization_barrier((text, columns[0]))
    text = jnp.concatenate([text, swap(text, "yl")], axis=0)
    spread_rows = []
    for column_in in columns:
        merged = jnp.dot(column_in, merge_weight, preferred_element_type=jnp.float32).astype(
            jnp.bfloat16
        )
        spread_rows.append(jnp.broadcast_to(merged[None], (DP_COUNT,) + merged.shape))
    text, spread_rows[1] = lax.optimization_barrier((text, spread_rows[1]))
    wholes = [lax.all_to_all(rows, DP, split_axis=0, concat_axis=0) for rows in spread_rows]
    gains = attn_gain.reshape(DP_COUNT, 1, -1)
    image_queries, image_kvs = [None, None], [None, None]
    image_queries[0], image_kvs[0] = project(wholes[0], gains, query_weight, kv_weight)
    first = jnp.concatenate(
        [image_kvs[0]]
        + [
            lax.ppermute(image_kvs[0], "z", [(i, (i + step) % 4) for i in range(4)])
            for step in (1, 2, 3)
        ],
        axis=0,
    )
    first = jnp.concatenate([first, swap(first, "yl")], axis=0)
    first_far, text_far = swap(first, "c"), swap(text, "c")
    first_far, text_far, wholes[1] = lax.optimization_barrier((first_far, text_far, wholes[1]))
    first = [half.reshape((8,) + image_kvs[0].shape) for half in (first, first_far)]
    text = [half.reshape(6, SEQ, -1) for half in (text, text_far)]
    image_queries[1], image_kvs[1] = project(wholes[1], gains, query_weight, kv_weight)

    sizes = jnp.swapaxes(facts[:, :, :4], 0, 1)
    offsets = jnp.swapaxes(facts[:, :, 4:8], 0, 1)
    starts = jnp.sum(facts[0, :, 8:], axis=0, dtype=jnp.int32)
    positions = row_positions(sizes.reshape(128, 4), offsets.reshape(128, 4), CAPACITY).reshape(
        16, 256
    )
    before = jnp.arange(256)[None, :] < jnp.arange(256)[:, None]
    own_owner = lax.dynamic_index_in_dim(positions, ctx_index, 0, False) // SEQ
    own_rank = jnp.sum(
        ((own_owner[None, :] == own_owner[:, None]) & before).astype(jnp.int32),
        axis=1,
        dtype=jnp.int32,
    )
    own_slot = (own_owner * CAPACITY + own_rank).reshape(8, 2, CHUNK).swapaxes(0, 1).reshape(-1)
    spread_out = (jnp.arange(512, dtype=jnp.int32)[:, None] == own_slot[None, :]).astype(
        jnp.bfloat16
    )
    mine = positions // SEQ == ctx_index
    rank = jnp.sum((mine[:, None, :] & before[None]).astype(jnp.int32), axis=2, dtype=jnp.int32)
    slot_here = mine[:, :, None] & (
        rank[:, :, None] == jnp.arange(CAPACITY, dtype=jnp.int32)[None, None, :]
    )
    slot_place = jnp.sum(
        jnp.where(slot_here, positions[:, :, None] - ctx_index * SEQ + 1, 0),
        axis=1,
        dtype=jnp.int32,
    ).reshape(-1) - 1
    bring_in = jnp.arange(SEQ, dtype=jnp.int32)[:, None] == slot_place[None, :]

    chunk_rows = DP_COUNT * CHUNK
    sent = sum(
        jnp.dot(
            spread_out[:, k * chunk_rows : (k + 1) * chunk_rows],
            image_queries[k],
            preferred_element_type=jnp.float32,
        )
        for k in (0, 1)
    ).astype(jnp.bfloat16)
    half = chunk_rows // 2
    folded = jnp.concatenate([image_kvs[1][:half], image_kvs[1][half:]], axis=1)
    last = lax.all_to_all(
        jnp.concatenate(
            [
                jnp.broadcast_to(folded[None], (CTX_COUNT,) + folded.shape),
                sent.reshape(CTX_COUNT, CAPACITY, -1),
            ],
            axis=1,
        ),
        CTX,
        split_axis=0,
        concat_axis=0,
    )

    window_start = jnp.maximum(ctx_index - REACH, 0) * SEQ
    low_rows = (
        jnp.sum(
            jnp.where(
                doc_ids[:, None] == jnp.arange(4, dtype=jnp.int32)[None, :], starts[None, :], 0
            ),
            axis=1,
            dtype=jnp.int32,
        )
        - window_start
    )
    low_rows = jnp.maximum(low_rows, 0)
    edges = low_rows.reshape(-1, QUERY_BLOCK)
    info = jnp.concatenate(
        [
            jnp.stack([window_start, ctx_index * SEQ - window_start]).astype(jnp.int32),
            jnp.stack([edges[:, 0], edges[:, -1]], axis=1).reshape(-1),
        ]
    )
    within_device = starts_within(sizes)
    block = jnp.arange(CTX_COUNT, dtype=jnp.int32)
    first_from = (
        (z_at - block % 4 + 4) % 4 * 4 + ((block // 4 % 2) ^ yl_at) * 2 + ((block // 8) ^ c_at)
    )
    shard = window_start // SEQ + jnp.arange(REACH + 1, dtype=jnp.int32)
    text_at = (
        ((shard % 2) ^ c_at) * 6
        + ((shard // 2 % 2) ^ yl_at) * 3
        + jnp.clip(z_at - shard // 4, 0, 2)
    )
    image_src = (
        jnp.arange(CTX_COUNT * DP_COUNT, dtype=jnp.int32).reshape(CTX_COUNT, DP_COUNT, 1) * CAPACITY
        + within_device
    )
    targets = (offsets - window_start).reshape(-1)
    inside = (targets >= 0) & (targets < WINDOW)
    tables = (
        info,
        image_src.reshape(-1),
        jnp.where(inside, targets, 0),
        jnp.where(inside, sizes.reshape(-1), 0),
        jnp.concatenate([first_from, text_at]).astype(jnp.int32),
    )
    return attention(
        tables, text_query, bring_in.astype(jnp.bfloat16), low_rows[None, :], first, last, text
    )


def solution(mesh):
    fine = Mesh(mesh.devices.reshape(2, 4, 4, 2, 2), DP + CTX)
    every = DP + CTX
    return jax.shard_map(
        body,
        mesh=fine,
        in_specs=(
            P(every, None),
            P(),
            P(),
            P(every, None),
            P(every, None),
            P(),
            P(),
            P(None, DP),
            P(),
            P(None, DP),
            P(None, None, DP),
            P(CTX, DP),
            P(None, CTX, DP),
            P(CTX),
            P(every, None),
            P(every, None),
        ),
        out_specs=P(CTX, DP),
        check_vma=False,
    )
```

profile of v0, /device:TPU:81, one launch (start us, length us, event | category | flops | bytes accessed | tf_op | source)
XLA Modules:
  0.0 315.5 jit_solution(8022115560364390535)
XLA Ops:
  8.5 6.7 %all-to-all-start = ((bf16[16,48,1280]{2,1,0:T(8,128)(2,1)}), bf16[16,48,1280]{2,1,0:T(8,128)(2,1)S(1)}, u32[]{:S(2)}, u32[]{:S(2)}) async-start(bf16[16,48,1280]{2,1,0:T(8,128)(2,1)} %broadcast_in_dim.67), calls=%async_computation | async-start | bytes 3932160 | tf_op jit(solution)/shard_map/all_to_all | solution.py:365
  15.6 8.1 %collective-permute-done = bf16[128,1280]{1,0:T(8,128)(2,1)} collective-permute-done((bf16[128,1280]{1,0:T(8,128)(2,1)S(1)}, bf16[128,1280]{1,0:T(8,128)(2,1)}, u32[]{:S(2)}, u32[]{:S(2)}) %collective-permute-start) | collective-permute-done | bytes 327712 | tf_op jit(solution)/shard_map/ppermute | solution.py:370
  29.8 11.5 %all-to-all-done = bf16[16,48,1280]{2,1,0:T(8,128)(2,1)S(1)} async-done(((bf16[16,48,1280]{2,1,0:T(8,128)(2,1)}), bf16[16,48,1280]{2,1,0:T(8,128)(2,1)S(1)}, u32[]{:S(2)}, u32[]{:S(2)}) %all-to-all-start) | async-done | bytes 1966112 | tf_op jit(solution)/shard_map/all_to_all | solution.py:365
  41.6 3.4 %multiply_convert_fusion = bf16[1024,384]{1,0:T(8,128)(2,1)S(1)} fusion(bf16[1024,1280]{1,0:T(8,128)(2,1)} %constant_dynamic-update-slice_fusion, bf16[384,1280]{1,0:T(8,128)(2,1)S(1)} %bitcast.84), kind=kOutput, calls=%fused_computation.8 | convolution fusion | flops 1008992256 | bytes 4390912 | tf_op jit(solution)/shard_map/dot_general | solution.py:381
  55.4 4.5 %all-to-all-start.1 = ((bf16[4,144,1280]{2,1,0:T(8,128)(2,1)}), bf16[4,144,1280]{2,1,0:T(8,128)(2,1)S(1)}, u32[]{:S(2)}, u32[]{:S(2)}) async-start(bf16[4,144,1280]{2,1,0:T(8,128)(2,1)} %pad_maximum_fusion.2), calls=%async_computation.1 | async-start | bytes 2949120 | tf_op jit(solution)/shard_map/all_to_all | solution.py:400
  60.2 17.3 %all-to-all-done.1 = bf16[4,144,1280]{2,1,0:T(8,128)(2,1)S(1)} async-done(((bf16[4,144,1280]{2,1,0:T(8,128)(2,1)}), bf16[4,144,1280]{2,1,0:T(8,128)(2,1)S(1)}, u32[]{:S(2)}, u32[]{:S(2)}) %all-to-all-start.1) | async-done | bytes 1474592 | tf_op jit(solution)/shard_map/all_to_all | solution.py:400
  79.9 3.7 %collective-permute-start.5 = (bf16[640,256]{1,0:T(8,128)(2,1)S(1)}, bf16[640,256]{1,0:T(8,128)(2,1)}, u32[]{:S(2)}, u32[]{:S(2)}) collective-permute-start(bf16[640,256]{1,0:T(8,128)(2,1)S(1)} %pad_maximum_fusion.9), channel_id=1, source_target_pairs={{0,4},{4,8},{8,12},{1,5},{5,9},{9,13},{2,6},{6,10},{10,14},{3,7},{... | collective-permute-start | bytes 983048 | tf_op jit(solution)/shard_map/ppermute | solution.py:426
  85.5 5.4 %all-to-all-start.2 = ((bf16[8,16,5120]{2,1,0:T(8,128)(2,1)}), bf16[8,16,5120]{2,1,0:T(8,128)(2,1)S(1)}, u32[]{:S(2)}, u32[]{:S(2)}) async-start(bf16[8,16,5120]{2,1,0:T(8,128)(2,1)} %broadcast_in_dim.84), calls=%async_computation.2 | async-start | bytes 2621440 | tf_op jit(solution)/shard_map/all_to_all | solution.py:63
  93.0 15.3 %all-to-all-done.2 = bf16[8,16,5120]{2,1,0:T(8,128)(2,1)S(1)} async-done(((bf16[8,16,5120]{2,1,0:T(8,128)(2,1)}), bf16[8,16,5120]{2,1,0:T(8,128)(2,1)S(1)}, u32[]{:S(2)}, u32[]{:S(2)}) %all-to-all-start.2) | async-done | bytes 1310752 | tf_op jit(solution)/shard_map/all_to_all | solution.py:63
  109.5 6.2 %all-to-all-start.4 = ((bf16[8,16,5120]{2,1,0:T(8,128)(2,1)}), bf16[8,16,5120]{2,1,0:T(8,128)(2,1)S(1)}, u32[]{:S(2)}, u32[]{:S(2)}) async-start(bf16[8,16,5120]{2,1,0:T(8,128)(2,1)} %broadcast_in_dim.86), calls=%async_computation.4 | async-start | bytes 2621440 | tf_op jit(solution)/shard_map/all_to_all | solution.py:63
  118.4 5.6 %convolution_convert_fusion.2 = bf16[128,1024]{1,0:T(8,128)(2,1)S(1)} fusion(bf16[128,5120]{1,0:T(8,128)(2,1)S(1)} %bitcast.75, bf16[5120,1024]{1,0:T(8,128)(2,1)} %param.23), kind=kOutput, calls=%fused_computation.17 | convolution fusion | flops 1342308352 | bytes 12058624 | tf_op jit(solution)/shard_map/dot_general | solution.py:439
  124.1 9.1 %all-to-all-done.4 = bf16[8,16,5120]{2,1,0:T(8,128)(2,1)S(1)} async-done(((bf16[8,16,5120]{2,1,0:T(8,128)(2,1)}), bf16[8,16,5120]{2,1,0:T(8,128)(2,1)S(1)}, u32[]{:S(2)}, u32[]{:S(2)}) %all-to-all-start.4) | async-done | bytes 1310752 | tf_op jit(solution)/shard_map/all_to_all | solution.py:63
  134.9 6.2 %all-to-all-start.3 = ((bf16[8,128,1024]{2,1,0:T(8,128)(2,1)}), bf16[8,128,1024]{2,1,0:T(8,128)(2,1)S(1)}, u32[]{:S(2)}, u32[]{:S(2)}) async-start(bf16[8,128,1024]{2,1,0:T(8,128)(2,1)} %broadcast_in_dim.85), calls=%async_computation.3 | async-start | bytes 4194304 | tf_op jit(solution)/shard_map/all_to_all | solution.py:444
  142.4 6.0 %convolution_convert_fusion.1 = bf16[128,1024]{1,0:T(8,128)(2,1)S(1)} fusion(bf16[128,5120]{1,0:T(8,128)(2,1)} %bitcast.76, bf16[5120,1024]{1,0:T(8,128)(2,1)} %param.23), kind=kOutput, calls=%fused_computation.16 | convolution fusion | flops 1342308352 | bytes 12058624 | tf_op jit(solution)/shard_map/dot_general | solution.py:439
  148.4 37.3 %collective-permute-done.12 = bf16[1920,256]{1,0:T(8,128)(2,1)S(1)} collective-permute-done((bf16[1920,256]{1,0:T(8,128)(2,1)}, bf16[1920,256]{1,0:T(8,128)(2,1)S(1)}, u32[]{:S(2)}, u32[]{:S(2)}) %collective-permute-start.12) | collective-permute-done | bytes 983072 | tf_op jit(solution)/shard_map/ppermute | solution.py:69
  191.9 6.6 %all-to-all-start.5 = ((bf16[8,128,1024]{2,1,0:T(8,128)(2,1)}), bf16[8,128,1024]{2,1,0:T(8,128)(2,1)S(1)}, u32[]{:S(2)}, u32[]{:S(2)}) async-start(bf16[8,128,1024]{2,1,0:T(8,128)(2,1)} %broadcast_in_dim.87), calls=%async_computation.5 | async-start | bytes 4194304 | tf_op jit(solution)/shard_map/all_to_all | solution.py:444
  199.2 3.4 %copy-done = bf16[8192,512]{1,0:T(8,128)(2,1)S(1)} copy-done((bf16[8192,512]{1,0:T(8,128)(2,1)S(1)}, bf16[8192,512]{1,0:T(8,128)(2,1)}, u32[]{:S(2)}) %copy-start) | copy-done | bytes 8388632
  206.4 4.2 %shard_map.154 = (bf16[128,512]{1,0:T(8,128)(2,1)S(1)}, bf16[128,256]{1,0:T(8,128)(2,1)S(1)}) custom-call(bf16[8,128,1024]{2,1,0:T(8,128)(2,1)S(1)} %copy-done.5, f32[8,1,1024]{2,1,0:T(1,128)S(1)} %bitcast.71, bf16[8192,512]{1,0:T(8,128)(2,1)S(1)} %copy-done, bf16[2,8192,128]{2,1,0:T(8,128)(2,1)S(1)} %copy-done.2), custom_call_target="tpu_custom_call" | custom-call | flops 1610612736 | bytes 14680064 | tf_op jit(solution)/shard_map/pallas_call | solution.py:292
  219.5 11.1 %collective-permute-done.10 = bf16[512,256]{1,0:T(8,128)(2,1)S(1)} collective-permute-done((bf16[512,256]{1,0:T(8,128)(2,1)S(1)}, bf16[512,256]{1,0:T(8,128)(2,1)S(1)}, u32[]{:S(2)}, u32[]{:S(2)}) %collective-permute-start.10) | collective-permute-done | bytes 262176 | tf_op jit(solution)/shard_map/ppermute | solution.py:69
  236.8 3.6 %copy-done.1 = bf16[8192,512]{1,0:T(8,128)(2,1)S(1)} copy-done((bf16[8192,512]{1,0:T(8,128)(2,1)S(1)}, bf16[8192,512]{1,0:T(8,128)(2,1)}, u32[]{:S(2)}) %copy-start.1) | copy-done | bytes 8388632
  242.6 4.2 %shard_map.155 = (bf16[128,512]{1,0:T(8,128)(2,1)S(1)}, bf16[128,256]{1,0:T(8,128)(2,1)S(1)}) custom-call(bf16[8,128,1024]{2,1,0:T(8,128)(2,1)S(1)} %all-to-all-done.5.rows_ref, f32[8,1,1024]{2,1,0:T(1,128)S(1)} %bitcast.72, bf16[8192,512]{1,0:T(8,128)(2,1)S(1)} %copy-done.1, bf16[2,8192,128]{2,1,0:T(8,128)(2,1)S(1)} %copy-done.3), custom_call_target="tpu_custom_call" | custom-call | flops 1610612736 | bytes 14680064 | tf_op jit(solution)/shard_map/pallas_call | solution.py:292
  248.6 8.0 %all-to-all-start.6 = ((bf16[16,96,512]{2,1,0:T(8,128)(2,1)}), bf16[16,96,512]{2,1,0:T(8,128)(2,1)S(1)}, u32[]{:S(2)}, u32[]{:S(2)}) async-start(bf16[16,96,512]{2,1,0:T(8,128)(2,1)} %pad_maximum_fusion.1), calls=%async_computation.6 | async-start | bytes 3145728 | tf_op jit(solution)/shard_map/all_to_all | solution.py:503
  259.7 16.2 %all-to-all-done.6.last_ref = bf16[16,96,512]{2,1,0:T(8,128)(2,1)S(1)} async-done(((bf16[16,96,512]{2,1,0:T(8,128)(2,1)}), bf16[16,96,512]{2,1,0:T(8,128)(2,1)S(1)}, u32[]{:S(2)}, u32[]{:S(2)}) %all-to-all-start.6) | async-done | bytes 1572896 | tf_op jit(solution)/shard_map/all_to_all | solution.py:503
  277.0 38.3 %shard_map.156 = bf16[640,512]{1,0:T(8,128)(2,1)} custom-call(s32[4]{0:T(128)S(1)} %pad_add_fusion.1.info, s32[512]{0:T(512)S(1)} %add.286.image_src, s32[512]{0:T(512)S(1)} %get-tuple-element.71.image_dst, s32[512]{0:T(512)S(1)} %get-tuple-element.70.image_len, s32[25]{0:T(128)S(1)} %pad_add_fusion.2.blocks_at, bf16[640,512]{1,0:T(8,128)(2,1)S(1)} %copy-done.7, ...), custom_call_target="tpu_custom_call" | custom-call | flops 8000000000 | bytes 8000000 | tf_op jit(solution)/shard_map/pallas_call | solution.py:243
  (186 shorter events, 72.7 us)
Async XLA Ops:
  5.3 9.9 %collective-permute-start.2 = (bf16[128,1280]{1,0:T(8,128)(2,1)S(1)}, bf16[128,1280]{1,0:T(8,128)(2,1)S(1)}, u32[]{:S(2)}, u32[]{:S(2)}) collective-permute-start(bf16[128,1280]{1,0:T(8,128)(2,1)S(1)} %get-tuple-element.42), channel_id=1, source_target_pairs={{0,12},{4,0},{8,4},{12,8},{1,13},{5,1},{9,5},{13,9},{2,14},{6,2},{... | collective-permute-start | bytes 983048 | tf_op jit(solution)/shard_map/ppermute | solution.py:370
  5.3 10.3 %collective-permute-start.1 = (bf16[128,1280]{1,0:T(8,128)(2,1)S(1)}, bf16[128,1280]{1,0:T(8,128)(2,1)S(1)}, u32[]{:S(2)}, u32[]{:S(2)}) collective-permute-start(bf16[128,1280]{1,0:T(8,128)(2,1)S(1)} %get-tuple-element.42), channel_id=1, source_target_pairs={{0,8},{4,12},{8,0},{12,4},{1,9},{5,13},{9,1},{13,5},{2,10},{6,14},... | collective-permute-start | bytes 983048 | tf_op jit(solution)/shard_map/ppermute | solution.py:370
  8.5 15.3 %collective-permute-start = (bf16[128,1280]{1,0:T(8,128)(2,1)S(1)}, bf16[128,1280]{1,0:T(8,128)(2,1)}, u32[]{:S(2)}, u32[]{:S(2)}) collective-permute-start(bf16[128,1280]{1,0:T(8,128)(2,1)S(1)} %get-tuple-element.42), channel_id=1, source_target_pairs={{0,4},{4,8},{8,12},{12,0},{1,5},{5,9},{9,13},{13,1},{2,6},{6,10},{... | collective-permute-start | bytes 983048 | tf_op jit(solution)/shard_map/ppermute | solution.py:370
  8.5 32.8 %all-to-all-start = ((bf16[16,48,1280]{2,1,0:T(8,128)(2,1)}), bf16[16,48,1280]{2,1,0:T(8,128)(2,1)S(1)}, u32[]{:S(2)}, u32[]{:S(2)}) async-start(bf16[16,48,1280]{2,1,0:T(8,128)(2,1)} %broadcast_in_dim.67), calls=%async_computation | async-start | bytes 3932160 | tf_op jit(solution)/shard_map/all_to_all | solution.py:365
  24.8 3.8 %collective-permute-start.3 = (bf16[512,1280]{1,0:T(8,128)(2,1)S(1)}, bf16[512,1280]{1,0:T(8,128)(2,1)S(1)}, u32[]{:S(2)}, u32[]{:S(2)}) collective-permute-start(bf16[512,1280]{1,0:T(8,128)(2,1)S(1)} %pad_maximum_fusion.3), channel_id=1, source_target_pairs={{0,1},{1,0},{2,3},{3,2},{4,5},{5,4},{6,7},{7,6},{8,9},{9,8},{10,11... | collective-permute-start | bytes 3932168 | tf_op jit(solution)/shard_map/ppermute | solution.py:69
  46.0 4.9 %collective-permute-start.4 = (bf16[528,1280]{1,0:T(8,128)(2,1)S(1)}, bf16[528,1280]{1,0:T(8,128)(2,1)}, u32[]{:S(2)}, u32[]{:S(2)}) collective-permute-start(bf16[528,1280]{1,0:T(8,128)(2,1)S(1)} %fusion.1), channel_id=1, source_target_pairs={{0,1},{1,0},{2,3},{3,2},{4,5},{5,4},{6,7},{7,6},{8,9},{9,8},{10,11... | collective-permute-start | bytes 4055048 | tf_op jit(solution)/shard_map/ppermute | solution.py:69
  55.4 22.0 %all-to-all-start.1 = ((bf16[4,144,1280]{2,1,0:T(8,128)(2,1)}), bf16[4,144,1280]{2,1,0:T(8,128)(2,1)S(1)}, u32[]{:S(2)}, u32[]{:S(2)}) async-start(bf16[4,144,1280]{2,1,0:T(8,128)(2,1)} %pad_maximum_fusion.2), calls=%async_computation.1 | async-start | bytes 2949120 | tf_op jit(solution)/shard_map/all_to_all | solution.py:400
  60.0 30.9 %copy-start.24 = (pred[4,4]{1,0:T(4,128)(4,1)}, pred[4,4]{1,0:T(4,128)(4,1)S(1)}, u32[]{:S(2)}) copy-start(pred[4,4]{1,0:T(4,128)(4,1)S(1)} %iota_compare_fusion.14) | copy-start | bytes 52
  78.6 37.8 %collective-permute-start.6 = (bf16[640,256]{1,0:T(8,128)(2,1)S(1)}, bf16[640,256]{1,0:T(8,128)(2,1)}, u32[]{:S(2)}, u32[]{:S(2)}) collective-permute-start(bf16[640,256]{1,0:T(8,128)(2,1)S(1)} %pad_maximum_fusion.9), channel_id=1, source_target_pairs={{0,8},{4,12},{1,9},{5,13},{2,10},{6,14},{3,11},{7,15},{16,24},{20,... | collective-permute-start | bytes 983048 | tf_op jit(solution)/shard_map/ppermute | solution.py:427
  79.9 36.5 %collective-permute-start.5 = (bf16[640,256]{1,0:T(8,128)(2,1)S(1)}, bf16[640,256]{1,0:T(8,128)(2,1)}, u32[]{:S(2)}, u32[]{:S(2)}) collective-permute-start(bf16[640,256]{1,0:T(8,128)(2,1)S(1)} %pad_maximum_fusion.9), channel_id=1, source_target_pairs={{0,4},{4,8},{8,12},{1,5},{5,9},{9,13},{2,6},{6,10},{10,14},{3,7},{... | collective-permute-start | bytes 983048 | tf_op jit(solution)/shard_map/ppermute | solution.py:426
  85.5 22.8 %all-to-all-start.2 = ((bf16[8,16,5120]{2,1,0:T(8,128)(2,1)}), bf16[8,16,5120]{2,1,0:T(8,128)(2,1)S(1)}, u32[]{:S(2)}, u32[]{:S(2)}) async-start(bf16[8,16,5120]{2,1,0:T(8,128)(2,1)} %broadcast_in_dim.84), calls=%async_computation.2 | async-start | bytes 2621440 | tf_op jit(solution)/shard_map/all_to_all | solution.py:63
  109.5 23.7 %all-to-all-start.4 = ((bf16[8,16,5120]{2,1,0:T(8,128)(2,1)}), bf16[8,16,5120]{2,1,0:T(8,128)(2,1)S(1)}, u32[]{:S(2)}, u32[]{:S(2)}) async-start(bf16[8,16,5120]{2,1,0:T(8,128)(2,1)} %broadcast_in_dim.86), calls=%async_computation.4 | async-start | bytes 2621440 | tf_op jit(solution)/shard_map/all_to_all | solution.py:63
  134.9 55.6 %all-to-all-start.3 = ((bf16[8,128,1024]{2,1,0:T(8,128)(2,1)}), bf16[8,128,1024]{2,1,0:T(8,128)(2,1)S(1)}, u32[]{:S(2)}, u32[]{:S(2)}) async-start(bf16[8,128,1024]{2,1,0:T(8,128)(2,1)} %broadcast_in_dim.85), calls=%async_computation.3 | async-start | bytes 4194304 | tf_op jit(solution)/shard_map/all_to_all | solution.py:444
  141.2 44.5 %collective-permute-start.12 = (bf16[1920,256]{1,0:T(8,128)(2,1)}, bf16[1920,256]{1,0:T(8,128)(2,1)S(1)}, u32[]{:S(2)}, u32[]{:S(2)}) collective-permute-start(bf16[1920,256]{1,0:T(8,128)(2,1)} %pad_maximum_fusion.4), channel_id=1, source_target_pairs={{0,2},{2,0},{1,3},{3,1},{4,6},{6,4},{5,7},{7,5},{8,10},{10,8},{9,1... | collective-permute-start | bytes 2949128 | tf_op jit(solution)/shard_map/ppermute | solution.py:69
  142.4 43.3 %copy-start.13 = (bf16[1920,256]{1,0:T(8,128)(2,1)S(1)}, bf16[1920,256]{1,0:T(8,128)(2,1)}, u32[]{:S(2)}) copy-start(bf16[1920,256]{1,0:T(8,128)(2,1)} %pad_maximum_fusion.4) | copy-start | bytes 2949124
  188.7 48.1 %collective-permute-start.13 = (bf16[3840,256]{1,0:T(8,128)(2,1)}, bf16[3840,256]{1,0:T(8,128)(2,1)}, u32[]{:S(2)}, u32[]{:S(2)}) collective-permute-start(bf16[3840,256]{1,0:T(8,128)(2,1)} %pad_maximum_fusion), channel_id=1, source_target_pairs={{0,1},{1,0},{2,3},{3,2},{4,5},{5,4},{6,7},{7,6},{8,9},{9,8},{10,11... | collective-permute-start | bytes 5898248 | tf_op jit(solution)/shard_map/ppermute | solution.py:69
  191.9 44.9 %all-to-all-start.5 = ((bf16[8,128,1024]{2,1,0:T(8,128)(2,1)}), bf16[8,128,1024]{2,1,0:T(8,128)(2,1)S(1)}, u32[]{:S(2)}, u32[]{:S(2)}) async-start(bf16[8,128,1024]{2,1,0:T(8,128)(2,1)} %broadcast_in_dim.87), calls=%async_computation.5 | async-start | bytes 4194304 | tf_op jit(solution)/shard_map/all_to_all | solution.py:444
  210.6 6.6 %collective-permute-start.9 = (bf16[128,256]{1,0:T(8,128)(2,1)S(1)}, bf16[128,256]{1,0:T(8,128)(2,1)S(1)}, u32[]{:S(2)}, u32[]{:S(2)}) collective-permute-start(bf16[128,256]{1,0:T(8,128)(2,1)S(1)} %get-tuple-element.25), channel_id=1, source_target_pairs={{0,12},{4,0},{8,4},{12,8},{1,13},{5,1},{9,5},{13,9},{2,14},{6,2},{... | collective-permute-start | bytes 196616 | tf_op jit(solution)/shard_map/ppermute | solution.py:451
  213.2 4.9 %collective-permute-start.8 = (bf16[128,256]{1,0:T(8,128)(2,1)S(1)}, bf16[128,256]{1,0:T(8,128)(2,1)S(1)}, u32[]{:S(2)}, u32[]{:S(2)}) collective-permute-start(bf16[128,256]{1,0:T(8,128)(2,1)S(1)} %get-tuple-element.25), channel_id=1, source_target_pairs={{0,8},{4,12},{8,0},{12,4},{1,9},{5,13},{9,1},{13,5},{2,10},{6,14},... | collective-permute-start | bytes 196616 | tf_op jit(solution)/shard_map/ppermute | solution.py:451
  215.2 3.7 %collective-permute-start.7 = (bf16[128,256]{1,0:T(8,128)(2,1)S(1)}, bf16[128,256]{1,0:T(8,128)(2,1)S(1)}, u32[]{:S(2)}, u32[]{:S(2)}) collective-permute-start(bf16[128,256]{1,0:T(8,128)(2,1)S(1)} %get-tuple-element.25), channel_id=1, source_target_pairs={{0,4},{4,8},{8,12},{12,0},{1,5},{5,9},{9,13},{13,1},{2,6},{6,10},{... | collective-permute-start | bytes 196616 | tf_op jit(solution)/shard_map/ppermute | solution.py:451
  218.8 11.8 %collective-permute-start.10 = (bf16[512,256]{1,0:T(8,128)(2,1)S(1)}, bf16[512,256]{1,0:T(8,128)(2,1)S(1)}, u32[]{:S(2)}, u32[]{:S(2)}) collective-permute-start(bf16[512,256]{1,0:T(8,128)(2,1)S(1)} %pad_maximum_fusion.10), channel_id=1, source_target_pairs={{0,2},{2,0},{1,3},{3,1},{4,6},{6,4},{5,7},{7,5},{8,10},{10,8},{9,1... | collective-permute-start | bytes 786440 | tf_op jit(solution)/shard_map/ppermute | solution.py:69
  230.7 6.1 %collective-permute-start.11 = (bf16[1024,256]{1,0:T(8,128)(2,1)S(1)}, bf16[1024,256]{1,0:T(8,128)(2,1)S(1)}, u32[]{:S(2)}, u32[]{:S(2)}) collective-permute-start(bf16[1024,256]{1,0:T(8,128)(2,1)S(1)} %constant_dynamic-update-slice_fusion.5), channel_id=1, source_target_pairs={{0,1},{1,0},{2,3},{3,2},{4,5},{5,4},{6,7},{7,6},{8,9},{9,8},{10,11... | collective-permute-start | bytes 1572872 | tf_op jit(solution)/shard_map/ppermute | solution.py:69
  248.6 27.4 %copy-start.7 = (bf16[640,512]{1,0:T(8,128)(2,1)S(1)}, bf16[640,512]{1,0:T(8,128)(2,1)}, u32[]{:S(2)}) copy-start(bf16[640,512]{1,0:T(8,128)(2,1)} %text_query_ref.1) | copy-start | bytes 1966084
  248.6 27.3 %all-to-all-start.6 = ((bf16[16,96,512]{2,1,0:T(8,128)(2,1)}), bf16[16,96,512]{2,1,0:T(8,128)(2,1)S(1)}, u32[]{:S(2)}, u32[]{:S(2)}) async-start(bf16[16,96,512]{2,1,0:T(8,128)(2,1)} %pad_maximum_fusion.1), calls=%async_computation.6 | async-start | bytes 3145728 | tf_op jit(solution)/shard_map/all_to_all | solution.py:503
  (23 other events, 135.9 us)
where the time goes:
time: 317 us; the launch traced here: 315 us
  waiting for transfers between devices  131 us (41%)
  starting transfers between devices  65.2 us (21%)
  Pallas kernels  46.7 us (15%)
  local copies, waits for them, and re-layouts  33.1 us (10%)
  matrix products  19.7 us (6%)
  other arithmetic  19.1 us (6%)
    ppermute x6, waiting for transfers between devices, swap(): return lax.ppermute(rows, axis, [(0, 1), (1, 0)])  51.3 us
    pallas_call x1, Pallas kernels, attention(): pl.pallas_call(attention_kernel, out_shape=jax.ShapeDtypeStruct(text_quer...  38.3 us
    all_to_all x2, waiting for transfers between devices, gather_by_exchange(): lax.all_to_all(jnp.broadcast_to(block[None], (count,) + block.shape), axe...  24.5 us
    unnamed x59, local copies, waits for them, and re-layouts  18.6 us
    all_to_all x1, waiting for transfers between devices, body(): lax.all_to_all(jnp.stack([jnp.concatenate([lax.dynamic_index_in_dim(by_z,...  17.3 us
    all_to_all x1, waiting for transfers between devices, body(): lax.all_to_all(jnp.concatenate([jnp.broadcast_to(folded[None], (CTX_COUNT...  16.2 us
    all_to_all x2, starting transfers between devices, body(): lax.all_to_all(rows, DP, split_axis=0, concat_axis=0)  12.9 us
    all_to_all x2, starting transfers between devices, gather_by_exchange(): lax.all_to_all(jnp.broadcast_to(block[None], (count,) + block.shape), axe...  11.6 us
  transfers between devices with their start and end apart: 21, of which 12 were waited for; matrix products, arithmetic and copies ran while one was open for 12% of the time, Pallas kernels for 1%

commit v1 on v0

--- a/solution.py
+++ b/solution.py
@@ -363,6 +363,9 @@
     block = jnp.broadcast_to(block[None], (16,) + block.shape)
     block, patches = lax.optimization_barrier((block, patches))
     units = lax.all_to_all(block, DP + ("yl",), split_axis=0, concat_axis=0)
+    text = jnp.concatenate([text_kv[0], text_kv[1]], axis=1)
+    text, units = lax.optimization_barrier((text, units))
+    text = jnp.concatenate([text, swap(text, "yl")], axis=0)
     normed = layer_norm(patches, vision_gain, vision_bias)
     column = jnp.concatenate(
         [normed]
@@ -418,7 +421,6 @@
     vision = (patches.astype(jnp.float32) + branch).astype(jnp.bfloat16)
     merged_in = layer_norm(vision, merge_gain, merge_bias).reshape(-1, 4 * width)
 
-    text = jnp.concatenate([text_kv[0], text_kv[1]], axis=1)
     text, merged_in = lax.optimization_barrier((text, merged_in))
     text = jnp.concatenate(
         [
@@ -432,8 +434,6 @@
         gather_by_exchange(merged_in[at : at + CHUNK], DP, DP_COUNT).reshape(-1, 4 * width)
         for at in (0, CHUNK)
     ]
-    text, columns[0] = lax.optimization_barrier((text, columns[0]))
-    text = jnp.concatenate([text, swap(text, "yl")], axis=0)
     spread_rows = []
     for column_in in columns:
         merged = jnp.dot(column_in, merge_weight, preferred_element_type=jnp.float32).astype(
@@ -540,8 +540,8 @@
     shard = window_start // SEQ + jnp.arange(REACH + 1, dtype=jnp.int32)
     text_at = (
         ((shard % 2) ^ c_at) * 6
-        + ((shard // 2 % 2) ^ yl_at) * 3
-        + jnp.clip(z_at - shard // 4, 0, 2)
+        + jnp.clip(z_at - shard // 4, 0, 2) * 2
+        + ((shard // 2 % 2) ^ yl_at)
     )
     image_src = (
         jnp.arange(CTX_COUNT * DP_COUNT, dtype=jnp.int32).reshape(CTX_COUNT, DP_COUNT, 1) * CAPACITY

time: 317 us -> 288 us (0.909)
  the two profiles are of different devices: /device:TPU:81 before, /device:TPU:121 now
where the time goes in v1:
time: 288 us; the launch traced here: 287 us
  waiting for transfers between devices  103 us (36%)
  starting transfers between devices  68.7 us (24%)
  Pallas kernels  41 us (14%)
  local copies, waits for them, and re-layouts  34.2 us (12%)
  matrix products  20.2 us (7%)
  other arithmetic  19.1 us (7%)
    pallas_call x1, Pallas kernels, attention(): pl.pallas_call(attention_kernel, out_shape=jax.ShapeDtypeStruct(text_quer...  32.6 us
    all_to_all x2, waiting for transfers between devices, gather_by_exchange(): lax.all_to_all(jnp.broadcast_to(block[None], (count,) + block.shape), axe...  25.6 us
    unnamed x59, local copies, waits for them, and re-layouts  18.4 us
    ppermute x6, waiting for transfers between devices, swap(): return lax.ppermute(rows, axis, [(0, 1), (1, 0)])  15.9 us
    all_to_all x1, waiting for transfers between devices, body(): lax.all_to_all(jnp.concatenate([jnp.broadcast_to(folded[None], (CTX_COUNT...  15.6 us
    all_to_all x2, starting transfers between devices, body(): lax.all_to_all(rows, DP, split_axis=0, concat_axis=0)  14.1 us
    all_to_all x2, waiting for transfers between devices, body(): lax.all_to_all(rows, DP, split_axis=0, concat_axis=0)  13.9 us
    dot_general x2, matrix products, body(): jnp.dot(column_in, merge_weight, preferred_element_type=jnp.float32)  11.9 us
  transfers between devices with their start and end apart: 21, of which 14 were waited for; matrix products, arithmetic and copies ran while one was open for 14% of the time, Pallas kernels for 1%

profile of v1, /device:TPU:121, one launch (start us, length us, event | category | flops | bytes accessed | tf_op | source)
XLA Modules:
  0.0 286.6 jit_solution(165040386514430084)
XLA Ops:
  8.0 6.6 %all-to-all-start = ((bf16[16,48,1280]{2,1,0:T(8,128)(2,1)}), bf16[16,48,1280]{2,1,0:T(8,128)(2,1)S(1)}, u32[]{:S(2)}, u32[]{:S(2)}) async-start(bf16[16,48,1280]{2,1,0:T(8,128)(2,1)} %broadcast_in_dim.67), calls=%async_computation | async-start | bytes 3932160 | tf_op jit(solution)/shard_map/all_to_all | solution.py:365
  14.6 7.5 %collective-permute-done.2 = bf16[128,1280]{1,0:T(8,128)(2,1)S(1)} collective-permute-done((bf16[128,1280]{1,0:T(8,128)(2,1)S(1)}, bf16[128,1280]{1,0:T(8,128)(2,1)S(1)}, u32[]{:S(2)}, u32[]{:S(2)}) %collective-permute-start.2) | collective-permute-done | bytes 327712 | tf_op jit(solution)/shard_map/ppermute | solution.py:373
  30.8 10.8 %all-to-all-done = bf16[16,48,1280]{2,1,0:T(8,128)(2,1)S(1)} async-done(((bf16[16,48,1280]{2,1,0:T(8,128)(2,1)}), bf16[16,48,1280]{2,1,0:T(8,128)(2,1)S(1)}, u32[]{:S(2)}, u32[]{:S(2)}) %all-to-all-start) | async-done | bytes 1966112 | tf_op jit(solution)/shard_map/all_to_all | solution.py:365
  42.8 3.7 %multiply_convert_fusion = bf16[1024,384]{1,0:T(8,128)(2,1)S(1)} fusion(bf16[1024,1280]{1,0:T(8,128)(2,1)} %constant_dynamic-update-slice_fusion, bf16[384,1280]{1,0:T(8,128)(2,1)} %bitcast.84), kind=kOutput, calls=%fused_computation.8 | convolution fusion | flops 1008992256 | bytes 4390912 | tf_op jit(solution)/shard_map/dot_general | solution.py:384
  56.7 4.4 %all-to-all-start.1 = ((bf16[4,144,1280]{2,1,0:T(8,128)(2,1)}), bf16[4,144,1280]{2,1,0:T(8,128)(2,1)S(1)}, u32[]{:S(2)}, u32[]{:S(2)}) async-start(bf16[4,144,1280]{2,1,0:T(8,128)(2,1)} %pad_maximum_fusion.2), calls=%async_computation.1 | async-start | bytes 2949120 | tf_op jit(solution)/shard_map/all_to_all | solution.py:403
  61.4 8.1 %collective-permute-done.5 = bf16[640,256]{1,0:T(8,128)(2,1)S(1)} collective-permute-done((bf16[640,256]{1,0:T(8,128)(2,1)S(1)}, bf16[640,256]{1,0:T(8,128)(2,1)S(1)}, u32[]{:S(2)}, u32[]{:S(2)}) %collective-permute-start.5) | collective-permute-done | bytes 327712 | tf_op jit(solution)/shard_map/ppermute | solution.py:69
  69.6 9.5 %all-to-all-done.1 = bf16[4,144,1280]{2,1,0:T(8,128)(2,1)S(1)} async-done(((bf16[4,144,1280]{2,1,0:T(8,128)(2,1)}), bf16[4,144,1280]{2,1,0:T(8,128)(2,1)S(1)}, u32[]{:S(2)}, u32[]{:S(2)}) %all-to-all-start.1) | async-done | bytes 1474592 | tf_op jit(solution)/shard_map/all_to_all | solution.py:403
  84.4 5.3 %all-to-all-start.2 = ((bf16[8,16,5120]{2,1,0:T(8,128)(2,1)}), bf16[8,16,5120]{2,1,0:T(8,128)(2,1)S(1)}, u32[]{:S(2)}, u32[]{:S(2)}) async-start(bf16[8,16,5120]{2,1,0:T(8,128)(2,1)} %broadcast_in_dim.84), calls=%async_computation.2 | async-start | bytes 2621440 | tf_op jit(solution)/shard_map/all_to_all | solution.py:63
  92.3 14.9 %all-to-all-done.2 = bf16[8,16,5120]{2,1,0:T(8,128)(2,1)S(1)} async-done(((bf16[8,16,5120]{2,1,0:T(8,128)(2,1)}), bf16[8,16,5120]{2,1,0:T(8,128)(2,1)S(1)}, u32[]{:S(2)}, u32[]{:S(2)}) %all-to-all-start.2) | async-done | bytes 1310752 | tf_op jit(solution)/shard_map/all_to_all | solution.py:63
  108.4 6.2 %all-to-all-start.4 = ((bf16[8,16,5120]{2,1,0:T(8,128)(2,1)}), bf16[8,16,5120]{2,1,0:T(8,128)(2,1)S(1)}, u32[]{:S(2)}, u32[]{:S(2)}) async-start(bf16[8,16,5120]{2,1,0:T(8,128)(2,1)} %broadcast_in_dim.86), calls=%async_computation.4 | async-start | bytes 2621440 | tf_op jit(solution)/shard_map/all_to_all | solution.py:63
  115.0 6.3 %convolution_convert_fusion.2 = bf16[128,1024]{1,0:T(8,128)(2,1)} fusion(bf16[128,5120]{1,0:T(8,128)(2,1)S(1)} %bitcast.75, bf16[5120,1024]{1,0:T(8,128)(2,1)} %param.23), kind=kOutput, calls=%fused_computation.17 | convolution fusion | flops 1342308352 | bytes 12058624 | tf_op jit(solution)/shard_map/dot_general | solution.py:439
  121.3 10.7 %all-to-all-done.4 = bf16[8,16,5120]{2,1,0:T(8,128)(2,1)S(1)} async-done(((bf16[8,16,5120]{2,1,0:T(8,128)(2,1)}), bf16[8,16,5120]{2,1,0:T(8,128)(2,1)S(1)}, u32[]{:S(2)}, u32[]{:S(2)}) %all-to-all-start.4) | async-done | bytes 1310752 | tf_op jit(solution)/shard_map/all_to_all | solution.py:63
  134.8 6.2 %all-to-all-start.3 = ((bf16[8,128,1024]{2,1,0:T(8,128)(2,1)}), bf16[8,128,1024]{2,1,0:T(8,128)(2,1)S(1)}, u32[]{:S(2)}, u32[]{:S(2)}) async-start(bf16[8,128,1024]{2,1,0:T(8,128)(2,1)} %broadcast_in_dim.85), calls=%async_computation.3 | async-start | bytes 4194304 | tf_op jit(solution)/shard_map/all_to_all | solution.py:444
  144.5 5.6 %convolution_convert_fusion.1 = bf16[128,1024]{1,0:T(8,128)(2,1)S(1)} fusion(bf16[128,5120]{1,0:T(8,128)(2,1)S(1)} %bitcast.76, bf16[5120,1024]{1,0:T(8,128)(2,1)} %param.23), kind=kOutput, calls=%fused_computation.16 | convolution fusion | flops 1342308352 | bytes 12058624 | tf_op jit(solution)/shard_map/dot_general | solution.py:439
  152.9 13.9 %all-to-all-done.3.rows_ref = bf16[8,128,1024]{2,1,0:T(8,128)(2,1)S(1)} async-done(((bf16[8,128,1024]{2,1,0:T(8,128)(2,1)}), bf16[8,128,1024]{2,1,0:T(8,128)(2,1)S(1)}, u32[]{:S(2)}, u32[]{:S(2)}) %all-to-all-start.3) | async-done | bytes 2097184 | tf_op jit(solution)/shard_map/all_to_all | solution.py:444
  168.2 7.9 %all-to-all-start.5 = ((bf16[8,128,1024]{2,1,0:T(8,128)(2,1)}), bf16[8,128,1024]{2,1,0:T(8,128)(2,1)S(1)}, u32[]{:S(2)}, u32[]{:S(2)}) async-start(bf16[8,128,1024]{2,1,0:T(8,128)(2,1)} %broadcast_in_dim.87), calls=%async_computation.5 | async-start | bytes 4194304 | tf_op jit(solution)/shard_map/all_to_all | solution.py:444
  184.6 4.2 %shard_map.154 = (bf16[128,512]{1,0:T(8,128)(2,1)S(1)}, bf16[128,256]{1,0:T(8,128)(2,1)S(1)}) custom-call(bf16[8,128,1024]{2,1,0:T(8,128)(2,1)S(1)} %copy-done.5, f32[8,1,1024]{2,1,0:T(1,128)S(1)} %bitcast.71, bf16[8192,512]{1,0:T(8,128)(2,1)S(1)} %copy-done, bf16[2,8192,128]{2,1,0:T(8,128)(2,1)S(1)} %copy-done.2), custom_call_target="tpu_custom_call" | custom-call | flops 1610612736 | bytes 14680064 | tf_op jit(solution)/shard_map/pallas_call | solution.py:292
  190.9 5.2 %collective-permute-start.7 = (bf16[128,256]{1,0:T(8,128)(2,1)S(1)}, bf16[128,256]{1,0:T(8,128)(2,1)S(1)}, u32[]{:S(2)}, u32[]{:S(2)}) collective-permute-start(bf16[128,256]{1,0:T(8,128)(2,1)S(1)} %get-tuple-element.25), channel_id=1, source_target_pairs={{0,8},{4,12},{8,0},{12,4},{1,9},{5,13},{9,1},{13,5},{2,10},{6,14},... | collective-permute-start | bytes 196616 | tf_op jit(solution)/shard_map/ppermute | solution.py:451
  200.3 4.9 %collective-permute-done.9 = bf16[512,256]{1,0:T(8,128)(2,1)S(1)} collective-permute-done((bf16[512,256]{1,0:T(8,128)(2,1)S(1)}, bf16[512,256]{1,0:T(8,128)(2,1)S(1)}, u32[]{:S(2)}, u32[]{:S(2)}) %collective-permute-start.9) | collective-permute-done | bytes 262176 | tf_op jit(solution)/shard_map/ppermute | solution.py:69
  205.2 4.7 %collective-permute-start.10 = (bf16[1024,256]{1,0:T(8,128)(2,1)S(1)}, bf16[1024,256]{1,0:T(8,128)(2,1)S(1)}, u32[]{:S(2)}, u32[]{:S(2)}) collective-permute-start(bf16[1024,256]{1,0:T(8,128)(2,1)S(1)} %constant_dynamic-update-slice_fusion.5), channel_id=1, source_target_pairs={{0,1},{1,0},{2,3},{3,2},{4,5},{5,4},{6,7},{7,6},{8,9},{9,8},{10,11... | collective-permute-start | bytes 1572872 | tf_op jit(solution)/shard_map/ppermute | solution.py:69
  219.3 4.2 %shard_map.155 = (bf16[128,512]{1,0:T(8,128)(2,1)S(1)}, bf16[128,256]{1,0:T(8,128)(2,1)S(1)}) custom-call(bf16[8,128,1024]{2,1,0:T(8,128)(2,1)S(1)} %all-to-all-done.5.rows_ref, f32[8,1,1024]{2,1,0:T(1,128)S(1)} %bitcast.72, bf16[8192,512]{1,0:T(8,128)(2,1)S(1)} %copy-done.1, bf16[2,8192,128]{2,1,0:T(8,128)(2,1)S(1)} %copy-done.3), custom_call_target="tpu_custom_call" | custom-call | flops 1610612736 | bytes 14680064 | tf_op jit(solution)/shard_map/pallas_call | solution.py:292
  225.3 9.1 %all-to-all-start.6 = ((bf16[16,96,512]{2,1,0:T(8,128)(2,1)}), bf16[16,96,512]{2,1,0:T(8,128)(2,1)S(1)}, u32[]{:S(2)}, u32[]{:S(2)}) async-start(bf16[16,96,512]{2,1,0:T(8,128)(2,1)} %pad_maximum_fusion.1), calls=%async_computation.6 | async-start | bytes 3145728 | tf_op jit(solution)/shard_map/all_to_all | solution.py:503
  237.3 15.6 %all-to-all-done.6.last_ref = bf16[16,96,512]{2,1,0:T(8,128)(2,1)S(1)} async-done(((bf16[16,96,512]{2,1,0:T(8,128)(2,1)}), bf16[16,96,512]{2,1,0:T(8,128)(2,1)S(1)}, u32[]{:S(2)}, u32[]{:S(2)}) %all-to-all-start.6) | async-done | bytes 1572896 | tf_op jit(solution)/shard_map/all_to_all | solution.py:503
  253.9 32.6 %shard_map.156 = bf16[640,512]{1,0:T(8,128)(2,1)} custom-call(s32[4]{0:T(128)S(1)} %pad_add_fusion.1.info, s32[512]{0:T(512)S(1)} %add.286.image_src, s32[512]{0:T(512)S(1)} %get-tuple-element.71.image_dst, s32[512]{0:T(512)S(1)} %get-tuple-element.70.image_len, s32[25]{0:T(128)S(1)} %pad_add_fusion.2.blocks_at, bf16[640,512]{1,0:T(8,128)(2,1)S(1)} %copy-done.7, ...), custom_call_target="tpu_custom_call" | custom-call | flops 8000000000 | bytes 8000000 | tf_op jit(solution)/shard_map/pallas_call | solution.py:243
  (186 shorter events, 77.7 us)
Async XLA Ops:
  5.3 16.8 %collective-permute-start.2 = (bf16[128,1280]{1,0:T(8,128)(2,1)S(1)}, bf16[128,1280]{1,0:T(8,128)(2,1)S(1)}, u32[]{:S(2)}, u32[]{:S(2)}) collective-permute-start(bf16[128,1280]{1,0:T(8,128)(2,1)S(1)} %get-tuple-element.42), channel_id=1, source_target_pairs={{0,12},{4,0},{8,4},{12,8},{1,13},{5,1},{9,5},{13,9},{2,14},{6,2},{... | collective-permute-start | bytes 983048 | tf_op jit(solution)/shard_map/ppermute | solution.py:373
  5.5 16.7 %collective-permute-start.1 = (bf16[128,1280]{1,0:T(8,128)(2,1)S(1)}, bf16[128,1280]{1,0:T(8,128)(2,1)S(1)}, u32[]{:S(2)}, u32[]{:S(2)}) collective-permute-start(bf16[128,1280]{1,0:T(8,128)(2,1)S(1)} %get-tuple-element.42), channel_id=1, source_target_pairs={{0,8},{4,12},{8,0},{12,4},{1,9},{5,13},{9,1},{13,5},{2,10},{6,14},... | collective-permute-start | bytes 983048 | tf_op jit(solution)/shard_map/ppermute | solution.py:373
  5.6 17.0 %collective-permute-start = (bf16[128,1280]{1,0:T(8,128)(2,1)S(1)}, bf16[128,1280]{1,0:T(8,128)(2,1)}, u32[]{:S(2)}, u32[]{:S(2)}) collective-permute-start(bf16[128,1280]{1,0:T(8,128)(2,1)S(1)} %get-tuple-element.42), channel_id=1, source_target_pairs={{0,4},{4,8},{8,12},{12,0},{1,5},{5,9},{9,13},{13,1},{2,6},{6,10},{... | collective-permute-start | bytes 983048 | tf_op jit(solution)/shard_map/ppermute | solution.py:373
  8.0 33.6 %all-to-all-start = ((bf16[16,48,1280]{2,1,0:T(8,128)(2,1)}), bf16[16,48,1280]{2,1,0:T(8,128)(2,1)S(1)}, u32[]{:S(2)}, u32[]{:S(2)}) async-start(bf16[16,48,1280]{2,1,0:T(8,128)(2,1)} %broadcast_in_dim.67), calls=%async_computation | async-start | bytes 3932160 | tf_op jit(solution)/shard_map/all_to_all | solution.py:365
  23.7 5.9 %collective-permute-start.3 = (bf16[512,1280]{1,0:T(8,128)(2,1)S(1)}, bf16[512,1280]{1,0:T(8,128)(2,1)S(1)}, u32[]{:S(2)}, u32[]{:S(2)}) collective-permute-start(bf16[512,1280]{1,0:T(8,128)(2,1)S(1)} %pad_maximum_fusion.3), channel_id=1, source_target_pairs={{0,1},{1,0},{2,3},{3,2},{4,5},{5,4},{6,7},{7,6},{8,9},{9,8},{10,11... | collective-permute-start | bytes 3932168 | tf_op jit(solution)/shard_map/ppermute | solution.py:69
  47.5 4.7 %collective-permute-start.4 = (bf16[528,1280]{1,0:T(8,128)(2,1)S(1)}, bf16[528,1280]{1,0:T(8,128)(2,1)}, u32[]{:S(2)}, u32[]{:S(2)}) collective-permute-start(bf16[528,1280]{1,0:T(8,128)(2,1)S(1)} %fusion.1), channel_id=1, source_target_pairs={{0,1},{1,0},{2,3},{3,2},{4,5},{5,4},{6,7},{7,6},{8,9},{9,8},{10,11... | collective-permute-start | bytes 4055048 | tf_op jit(solution)/shard_map/ppermute | solution.py:69
  56.7 22.4 %all-to-all-start.1 = ((bf16[4,144,1280]{2,1,0:T(8,128)(2,1)}), bf16[4,144,1280]{2,1,0:T(8,128)(2,1)S(1)}, u32[]{:S(2)}, u32[]{:S(2)}) async-start(bf16[4,144,1280]{2,1,0:T(8,128)(2,1)} %pad_maximum_fusion.2), calls=%async_computation.1 | async-start | bytes 2949120 | tf_op jit(solution)/shard_map/all_to_all | solution.py:403
  61.1 28.9 %copy-start.24 = (pred[4,4]{1,0:T(4,128)(4,1)}, pred[4,4]{1,0:T(4,128)(4,1)S(1)}, u32[]{:S(2)}) copy-start(pred[4,4]{1,0:T(4,128)(4,1)S(1)} %iota_compare_fusion.14) | copy-start | bytes 52
  61.1 8.4 %collective-permute-start.5 = (bf16[640,256]{1,0:T(8,128)(2,1)S(1)}, bf16[640,256]{1,0:T(8,128)(2,1)S(1)}, u32[]{:S(2)}, u32[]{:S(2)}) collective-permute-start(bf16[640,256]{1,0:T(8,128)(2,1)S(1)} %copy-done.14), channel_id=1, source_target_pairs={{0,2},{2,0},{1,3},{3,1},{4,6},{6,4},{5,7},{7,5},{8,10},{10,8},{9,1... | collective-permute-start | bytes 983048 | tf_op jit(solution)/shard_map/ppermute | solution.py:69
  80.2 61.5 %collective-permute-start.12 = (bf16[1280,256]{1,0:T(8,128)(2,1)S(1)}, bf16[1280,256]{1,0:T(8,128)(2,1)}, u32[]{:S(2)}, u32[]{:S(2)}) collective-permute-start(bf16[1280,256]{1,0:T(8,128)(2,1)S(1)} %pad_maximum_fusion.8), channel_id=1, source_target_pairs={{0,8},{4,12},{1,9},{5,13},{2,10},{6,14},{3,11},{7,15},{16,24},{20,... | collective-permute-start | bytes 1966088 | tf_op jit(solution)/shard_map/ppermute | solution.py:429
  81.5 60.2 %collective-permute-start.11 = (bf16[1280,256]{1,0:T(8,128)(2,1)S(1)}, bf16[1280,256]{1,0:T(8,128)(2,1)}, u32[]{:S(2)}, u32[]{:S(2)}) collective-permute-start(bf16[1280,256]{1,0:T(8,128)(2,1)S(1)} %pad_maximum_fusion.8), channel_id=1, source_target_pairs={{0,4},{4,8},{8,12},{1,5},{5,9},{9,13},{2,6},{6,10},{10,14},{3,7},{... | collective-permute-start | bytes 1966088 | tf_op jit(solution)/shard_map/ppermute | solution.py:428
  84.4 22.7 %all-to-all-start.2 = ((bf16[8,16,5120]{2,1,0:T(8,128)(2,1)}), bf16[8,16,5120]{2,1,0:T(8,128)(2,1)S(1)}, u32[]{:S(2)}, u32[]{:S(2)}) async-start(bf16[8,16,5120]{2,1,0:T(8,128)(2,1)} %broadcast_in_dim.84), calls=%async_computation.2 | async-start | bytes 2621440 | tf_op jit(solution)/shard_map/all_to_all | solution.py:63
  108.4 23.7 %all-to-all-start.4 = ((bf16[8,16,5120]{2,1,0:T(8,128)(2,1)}), bf16[8,16,5120]{2,1,0:T(8,128)(2,1)S(1)}, u32[]{:S(2)}, u32[]{:S(2)}) async-start(bf16[8,16,5120]{2,1,0:T(8,128)(2,1)} %broadcast_in_dim.86), calls=%async_computation.4 | async-start | bytes 2621440 | tf_op jit(solution)/shard_map/all_to_all | solution.py:63
  134.8 32.1 %all-to-all-start.3 = ((bf16[8,128,1024]{2,1,0:T(8,128)(2,1)}), bf16[8,128,1024]{2,1,0:T(8,128)(2,1)S(1)}, u32[]{:S(2)}, u32[]{:S(2)}) async-start(bf16[8,128,1024]{2,1,0:T(8,128)(2,1)} %broadcast_in_dim.85), calls=%async_computation.3 | async-start | bytes 4194304 | tf_op jit(solution)/shard_map/all_to_all | solution.py:444
  151.7 62.0 %collective-permute-start.13 = (bf16[3840,256]{1,0:T(8,128)(2,1)}, bf16[3840,256]{1,0:T(8,128)(2,1)}, u32[]{:S(2)}, u32[]{:S(2)}) collective-permute-start(bf16[3840,256]{1,0:T(8,128)(2,1)} %pad_maximum_fusion), channel_id=1, source_target_pairs={{0,1},{1,0},{2,3},{3,2},{4,5},{5,4},{6,7},{7,6},{8,9},{9,8},{10,11... | collective-permute-start | bytes 5898248 | tf_op jit(solution)/shard_map/ppermute | solution.py:69
  168.2 45.5 %all-to-all-start.5 = ((bf16[8,128,1024]{2,1,0:T(8,128)(2,1)}), bf16[8,128,1024]{2,1,0:T(8,128)(2,1)S(1)}, u32[]{:S(2)}, u32[]{:S(2)}) async-start(bf16[8,128,1024]{2,1,0:T(8,128)(2,1)} %broadcast_in_dim.87), calls=%async_computation.5 | async-start | bytes 4194304 | tf_op jit(solution)/shard_map/all_to_all | solution.py:444
  184.6 26.9 %copy-start.16 = (s32[16,8,4]{2,1,0:T(8,128)S(1)}, s32[16,8,4]{2,1,0:T(8,128)}, u32[]{:S(2)}) copy-start(s32[16,8,4]{2,1,0:T(8,128)} %bitcast_subtract_fusion) | copy-start | bytes 6148
  188.8 8.1 %collective-permute-start.8 = (bf16[128,256]{1,0:T(8,128)(2,1)S(1)}, bf16[128,256]{1,0:T(8,128)(2,1)S(1)}, u32[]{:S(2)}, u32[]{:S(2)}) collective-permute-start(bf16[128,256]{1,0:T(8,128)(2,1)S(1)} %get-tuple-element.25), channel_id=1, source_target_pairs={{0,12},{4,0},{8,4},{12,8},{1,13},{5,1},{9,5},{13,9},{2,14},{6,2},{... | collective-permute-start | bytes 196616 | tf_op jit(solution)/shard_map/ppermute | solution.py:451
  190.9 7.9 %collective-permute-start.7 = (bf16[128,256]{1,0:T(8,128)(2,1)S(1)}, bf16[128,256]{1,0:T(8,128)(2,1)S(1)}, u32[]{:S(2)}, u32[]{:S(2)}) collective-permute-start(bf16[128,256]{1,0:T(8,128)(2,1)S(1)} %get-tuple-element.25), channel_id=1, source_target_pairs={{0,8},{4,12},{8,0},{12,4},{1,9},{5,13},{9,1},{13,5},{2,10},{6,14},... | collective-permute-start | bytes 196616 | tf_op jit(solution)/shard_map/ppermute | solution.py:451
  196.2 3.4 %collective-permute-start.6 = (bf16[128,256]{1,0:T(8,128)(2,1)S(1)}, bf16[128,256]{1,0:T(8,128)(2,1)S(1)}, u32[]{:S(2)}, u32[]{:S(2)}) collective-permute-start(bf16[128,256]{1,0:T(8,128)(2,1)S(1)} %get-tuple-element.25), channel_id=1, source_target_pairs={{0,4},{4,8},{8,12},{12,0},{1,5},{5,9},{9,13},{13,1},{2,6},{6,10},{... | collective-permute-start | bytes 196616 | tf_op jit(solution)/shard_map/ppermute | solution.py:451
  199.6 5.6 %collective-permute-start.9 = (bf16[512,256]{1,0:T(8,128)(2,1)S(1)}, bf16[512,256]{1,0:T(8,128)(2,1)S(1)}, u32[]{:S(2)}, u32[]{:S(2)}) collective-permute-start(bf16[512,256]{1,0:T(8,128)(2,1)S(1)} %pad_maximum_fusion.10), channel_id=1, source_target_pairs={{0,2},{2,0},{1,3},{3,1},{4,6},{6,4},{5,7},{7,5},{8,10},{10,8},{9,1... | collective-permute-start | bytes 786440 | tf_op jit(solution)/shard_map/ppermute | solution.py:69
  205.2 8.5 %collective-permute-start.10 = (bf16[1024,256]{1,0:T(8,128)(2,1)S(1)}, bf16[1024,256]{1,0:T(8,128)(2,1)S(1)}, u32[]{:S(2)}, u32[]{:S(2)}) collective-permute-start(bf16[1024,256]{1,0:T(8,128)(2,1)S(1)} %constant_dynamic-update-slice_fusion.5), channel_id=1, source_target_pairs={{0,1},{1,0},{2,3},{3,2},{4,5},{5,4},{6,7},{7,6},{8,9},{9,8},{10,11... | collective-permute-start | bytes 1572872 | tf_op jit(solution)/shard_map/ppermute | solution.py:69
  225.3 27.6 %copy-start.7 = (bf16[640,512]{1,0:T(8,128)(2,1)S(1)}, bf16[640,512]{1,0:T(8,128)(2,1)}, u32[]{:S(2)}) copy-start(bf16[640,512]{1,0:T(8,128)(2,1)} %text_query_ref.1) | copy-start | bytes 1966084
  225.3 27.6 %all-to-all-start.6 = ((bf16[16,96,512]{2,1,0:T(8,128)(2,1)}), bf16[16,96,512]{2,1,0:T(8,128)(2,1)S(1)}, u32[]{:S(2)}, u32[]{:S(2)}) async-start(bf16[16,96,512]{2,1,0:T(8,128)(2,1)} %pad_maximum_fusion.1), calls=%async_computation.6 | async-start | bytes 3145728 | tf_op jit(solution)/shard_map/all_to_all | solution.py:503
  (23 other events, 121.7 us)

commit v2 on v1

--- a/solution.py
+++ b/solution.py
@@ -69,6 +69,17 @@
     return lax.ppermute(rows, axis, [(0, 1), (1, 0)])
 
 
+def turn(rows, axis, by):
+    return lax.ppermute(rows, axis, [(i, (i + by) % 4) for i in range(4)])
+
+
+def gather_by_ring(block):
+    pair = jnp.stack([block, swap(block, "yh")])
+    left, right = turn(pair, "x", 1), turn(pair, "x", -1)
+    across = jnp.stack([turn(left[0], "x", 1), turn(right[1], "x", -1)])
+    return jnp.concatenate([pair, left, right, across], axis=0)
+
+
 def attention_kernel(
     info,
     image_src,
@@ -78,8 +89,7 @@
     text_query_ref,
     bring_ref,
     low_ref,
-    first_near_ref,
-    first_far_ref,
+    first_ref,
     last_ref,
     text_near_ref,
     text_far_ref,
@@ -95,11 +105,10 @@
     sems,
 ):
     query_offset = info[1]
-    half = CTX_COUNT // 2
     near = text_near_ref.shape[0]
     copies = []
     for shard in range(REACH + 1):
-        at = blocks_at[CTX_COUNT + shard]
+        at = blocks_at[shard]
         target = text_held.at[pl.ds(shard * SEQ, SEQ), :]
 
         @pl.when(at < near)
@@ -112,21 +121,16 @@
 
         copies.append(pltpu.make_async_copy(text_near_ref.at[0], target, sems.at[shard]))
 
-    for side, first_ref in enumerate((first_near_ref, first_far_ref)):
-
-        def widen_first(block, unused, side=side, first_ref=first_ref):
-            source = blocks_at[side * half + block]
-            for device in range(DP_COUNT):
-                base = source * (DP_COUNT * CAPACITY) + device * CAPACITY
-                rows = pl.ds(pl.multiple_of(base, CHUNK), CHUNK)
-                held = first_ref[block, device * CHUNK : (device + 1) * CHUNK, :].astype(
-                    jnp.float32
-                )
-                image_key[rows, :] = held[:, :HEAD_DIM]
-                image_value[rows, :] = held[:, HEAD_DIM:]
-            return unused
-
-        lax.fori_loop(0, half, widen_first, 0)
+    def widen_first(source, unused):
+        for device in range(DP_COUNT):
+            base = source * (DP_COUNT * CAPACITY) + device * CAPACITY
+            rows = pl.ds(pl.multiple_of(base, CHUNK), CHUNK)
+            held = first_ref[source, device * CHUNK : (device + 1) * CHUNK, :].astype(jnp.float32)
+            image_key[rows, :] = held[:, :HEAD_DIM]
+            image_value[rows, :] = held[:, HEAD_DIM:]
+        return unused
+
+    lax.fori_loop(0, CTX_COUNT, widen_first, 0)
 
     def widen_last(source, unused):
         for device in range(DP_COUNT):
@@ -243,7 +247,7 @@
     return pl.pallas_call(
         attention_kernel,
         out_shape=jax.ShapeDtypeStruct(text_query.shape, jnp.bfloat16),
-        in_specs=[smem] * 5 + [vmem] * 6 + [pl.BlockSpec(memory_space=pl.ANY)] * 2,
+        in_specs=[smem] * 5 + [vmem] * 5 + [pl.BlockSpec(memory_space=pl.ANY)] * 2,
         out_specs=vmem,
         scratch_shapes=[
             pltpu.VMEM((WINDOW, 2 * HEAD_DIM), jnp.bfloat16),
@@ -260,10 +264,10 @@
         cost_estimate=pl.CostEstimate(
             flops=8_000_000_000, bytes_accessed=8_000_000, transcendentals=13_000_000
         ),
-    )(*tables, text_query, bring_in, low_rows, *first, last, *text)
-
-
-def project_kernel(rows_ref, gain_ref, query_weight_ref, kv_weight_ref, query_ref, kv_ref, query_sum, kv_sum, squares):
+    )(*tables, text_query, bring_in, low_rows, first, last, *text)
+
+
+def project_kernel(order_ref, rows_ref, gain_ref, query_weight_ref, kv_weight_ref, query_ref, kv_ref, query_sum, kv_sum, squares):
     step = pl.program_id(0)
 
     @pl.when(step == 0)
@@ -286,38 +290,41 @@
         kv_ref[...] = (kv_sum[...] * scale).astype(jnp.bfloat16)
 
 
-def project(whole, gain, query_weight, kv_weight):
+def project(order, whole, gain, query_weight, kv_weight):
     count, rows, part = whole.shape
     query_width, kv_width = query_weight.shape[1], kv_weight.shape[2]
     return pl.pallas_call(
         project_kernel,
-        grid=(count,),
+        grid_spec=pltpu.PrefetchScalarGridSpec(
+            num_scalar_prefetch=1,
+            grid=(count,),
+            in_specs=[
+                pl.BlockSpec((1, rows, part), lambda k, order: (k, 0, 0)),
+                pl.BlockSpec((1, 1, part), lambda k, order: (order[k], 0, 0)),
+                pl.BlockSpec((part, query_width), lambda k, order: (order[k], 0)),
+                pl.BlockSpec((2, part, kv_width), lambda k, order: (0, order[k], 0)),
+            ],
+            out_specs=(
+                pl.BlockSpec((rows, query_width), lambda k, order: (0, 0)),
+                pl.BlockSpec((rows, 2 * kv_width), lambda k, order: (0, 0)),
+            ),
+            scratch_shapes=[
+                pltpu.VMEM((rows, query_width), jnp.float32),
+                pltpu.VMEM((rows, 2 * kv_width), jnp.float32),
+                pltpu.VMEM((rows, 1), jnp.float32),
+            ],
+        ),
         out_shape=(
             jax.ShapeDtypeStruct((rows, query_width), jnp.bfloat16),
             jax.ShapeDtypeStruct((rows, 2 * kv_width), jnp.bfloat16),
         ),
-        in_specs=[
-            pl.BlockSpec((1, rows, part), lambda k: (k, 0, 0)),
-            pl.BlockSpec((1, 1, part), lambda k: (k, 0, 0)),
-            pl.BlockSpec((part, query_width), lambda k: (k, 0)),
-            pl.BlockSpec((2, part, kv_width), lambda k: (0, k, 0)),
-        ],
-        out_specs=(
-            pl.BlockSpec((rows, query_width), lambda k: (0, 0)),
-            pl.BlockSpec((rows, 2 * kv_width), lambda k: (0, 0)),
-        ),
-        scratch_shapes=[
-            pltpu.VMEM((rows, query_width), jnp.float32),
-            pltpu.VMEM((rows, 2 * kv_width), jnp.float32),
-            pltpu.VMEM((rows, 1), jnp.float32),
-        ],
-        compiler_params=pltpu.CompilerParams(vmem_limit_bytes=24 * 1024 * 1024),
+        compiler_params=pltpu.CompilerParams(vmem_limit_bytes=52 * 1024 * 1024),
         cost_estimate=pl.CostEstimate(
             flops=2 * rows * count * part * (query_width + 2 * kv_width),
             bytes_accessed=2 * count * part * (query_width + 2 * kv_width + rows),
             transcendentals=0,
         ),
-    )(whole, gain, query_weight, kv_weight)
+    )(order, whole, gain, query_weight, kv_weight)
 
 
 def body(
@@ -430,35 +437,38 @@
         ],
         axis=0,
     )
+    yh_at, x_at = lax.axis_index("yh"), lax.axis_index("x")
+    step = jnp.array([0, 0, 3, 3, 1, 1, 2, 2], jnp.int32)
+    order = (yh_at ^ (jnp.arange(8, dtype=jnp.int32) % 2)) * 4 + (x_at + step) % 4
+    member = jnp.arange(8, dtype=jnp.int32)
+    slot_of = jnp.sum(
+        jnp.where(member[:, None] == order[None, :], member[None, :], 0), axis=1, dtype=jnp.int32
+    )
     columns = [
-        gather_by_exchange(merged_in[at : at + CHUNK], DP, DP_COUNT).reshape(-1, 4 * width)
-        for at in (0, CHUNK)
+        gather_by_ring(merged_in[at : at + CHUNK]).reshape(-1, 4 * width) for at in (0, CHUNK)
     ]
     spread_rows = []
     for column_in in columns:
         merged = jnp.dot(column_in, merge_weight, preferred_element_type=jnp.float32).astype(
             jnp.bfloat16
         )
-        spread_rows.append(jnp.broadcast_to(merged[None], (DP_COUNT,) + merged.shape))
+        by_member = merged.reshape(DP_COUNT, CHUNK, -1)
+        spread_rows.append(
+            jnp.concatenate(
+                [lax.dynamic_index_in_dim(by_member, slot_of[d], 0, False) for d in range(8)],
+                axis=0,
+            )
+        )
     text, spread_rows[1] = lax.optimization_barrier((text, spread_rows[1]))
-    wholes = [lax.all_to_all(rows, DP, split_axis=0, concat_axis=0) for rows in spread_rows]
+    wholes = [gather_by_ring(rows) for rows in spread_rows]
     gains = attn_gain.reshape(DP_COUNT, 1, -1)
     image_queries, image_kvs = [None, None], [None, None]
-    image_queries[0], image_kvs[0] = project(wholes[0], gains, query_weight, kv_weight)
-    first = jnp.concatenate(
-        [image_kvs[0]]
-        + [
-            lax.ppermute(image_kvs[0], "z", [(i, (i + step) % 4) for i in range(4)])
-            for step in (1, 2, 3)
-        ],
-        axis=0,
-    )
-    first = jnp.concatenate([first, swap(first, "yl")], axis=0)
-    first_far, text_far = swap(first, "c"), swap(text, "c")
-    first_far, text_far, wholes[1] = lax.optimization_barrier((first_far, text_far, wholes[1]))
-    first = [half.reshape((8,) + image_kvs[0].shape) for half in (first, first_far)]
+    image_queries[0], image_kvs[0] = project(order, wholes[0], gains, query_weight, kv_weight)
+    first = gather_by_exchange(image_kvs[0], CTX, CTX_COUNT)
+    text_far = swap(text, "c")
+    first, text_far, wholes[1] = lax.optimization_barrier((first, text_far, wholes[1]))
     text = [half.reshape(6, SEQ, -1) for half in (text, text_far)]
-    image_queries[1], image_kvs[1] = project(wholes[1], gains, query_weight, kv_weight)
+    image_queries[1], image_kvs[1] = project(order, wholes[1], gains, query_weight, kv_weight)
 
     sizes = jnp.swapaxes(facts[:, :, :4], 0, 1)
     offsets = jnp.swapaxes(facts[:, :, 4:8], 0, 1)
@@ -533,10 +543,6 @@
         ]
     )
     within_device = starts_within(sizes)
-    block = jnp.arange(CTX_COUNT, dtype=jnp.int32)
-    first_from = (
-        (z_at - block % 4 + 4) % 4 * 4 + ((block // 4 % 2) ^ yl_at) * 2 + ((block // 8) ^ c_at)
-    )
     shard = window_start // SEQ + jnp.arange(REACH + 1, dtype=jnp.int32)
     text_at = (
         ((shard % 2) ^ c_at) * 6
@@ -554,7 +560,7 @@
         image_src.reshape(-1),
         jnp.where(inside, targets, 0),
         jnp.where(inside, sizes.reshape(-1), 0),
-        jnp.concatenate([first_from, text_at]).astype(jnp.int32),
+        text_at.astype(jnp.int32),
     )
     return attention(
         tables, text_query, bring_in.astype(jnp.bfloat16), low_rows[None, :], first, last, text

time: 288 us -> 291 us (1.010)
  the two profiles are of different devices: /device:TPU:121 before, /device:TPU:41 now
where the time goes in v2:
time: 291 us; the launch traced here: 290 us
  starting transfers between devices  78.9 us (27%)
  waiting for transfers between devices  70.3 us (24%)
  Pallas kernels  50.8 us (17%)
  local copies, waits for them, and re-layouts  33.4 us (11%)
  other arithmetic  25.4 us (9%)
  between operations  16 us (5%)
  matrix products  15 us (5%)
    pallas_call x1, Pallas kernels, attention(): pl.pallas_call(attention_kernel, out_shape=jax.ShapeDtypeStruct(text_quer...  32.2 us
    ppermute x16, waiting for transfers between devices, turn(): return lax.ppermute(rows, axis, [(i, (i + by) % 4) for i in range(4)])  25.3 us
    ppermute x8, starting transfers between devices, swap(): return lax.ppermute(rows, axis, [(0, 1), (1, 0)])  22.2 us
    pallas_call x2, Pallas kernels, project(): pl.pallas_call(project_kernel, grid_spec=pltpu.PrefetchScalarGridSpec(num...  18.6 us
    ppermute x16, starting transfers between devices, turn(): return lax.ppermute(rows, axis, [(i, (i + by) % 4) for i in range(4)])  18.4 us
    unnamed x87, local copies, waits for them, and re-layouts  17.9 us
    ppermute x8, waiting for transfers between devices, swap(): return lax.ppermute(rows, axis, [(0, 1), (1, 0)])  14.8 us
    all_to_all x1, waiting for transfers between devices, body(): units = lax.all_to_all(block, DP + ('yl',), split_axis=0, concat_axis=0)  10.2 us
  transfers between devices with their start and end apart: 33, of which 15 were waited for; matrix products, arithmetic and copies ran while one was open for 15% of the time, Pallas kernels for 3%

profile of v2, /device:TPU:41, one launch (start us, length us, event | category | flops | bytes accessed | tf_op | source)
XLA Modules:
  0.0 289.9 jit_solution(17743651764022218098)
XLA Ops:
  10.1 6.8 %all-to-all-start = ((bf16[16,48,1280]{2,1,0:T(8,128)(2,1)}), bf16[16,48,1280]{2,1,0:T(8,128)(2,1)S(1)}, u32[]{:S(2)}, u32[]{:S(2)}) async-start(bf16[16,48,1280]{2,1,0:T(8,128)(2,1)} %broadcast_in_dim.73), calls=%async_computation | async-start | bytes 3932160 | tf_op jit(solution)/shard_map/all_to_all | solution.py:372
  17.0 7.3 %collective-permute-done.2 = bf16[128,1280]{1,0:T(8,128)(2,1)} collective-permute-done((bf16[128,1280]{1,0:T(8,128)(2,1)S(1)}, bf16[128,1280]{1,0:T(8,128)(2,1)}, u32[]{:S(2)}, u32[]{:S(2)}) %collective-permute-start.2) | collective-permute-done | bytes 327712 | tf_op jit(solution)/shard_map/ppermute | solution.py:380
  31.7 10.2 %all-to-all-done = bf16[16,48,1280]{2,1,0:T(8,128)(2,1)S(1)} async-done(((bf16[16,48,1280]{2,1,0:T(8,128)(2,1)}), bf16[16,48,1280]{2,1,0:T(8,128)(2,1)S(1)}, u32[]{:S(2)}, u32[]{:S(2)}) %all-to-all-start) | async-done | bytes 1966112 | tf_op jit(solution)/shard_map/all_to_all | solution.py:372
  43.1 3.7 %multiply_convert_fusion = bf16[1024,384]{1,0:T(8,128)(2,1)S(1)} fusion(bf16[1024,1280]{1,0:T(8,128)(2,1)} %constant_dynamic-update-slice_fusion, bf16[384,1280]{1,0:T(8,128)(2,1)} %bitcast.195), kind=kOutput, calls=%fused_computation.8 | convolution fusion | flops 1008992256 | bytes 4390912 | tf_op jit(solution)/shard_map/dot_general | solution.py:391
  47.7 4.4 %collective-permute-start.4 = (bf16[528,1280]{1,0:T(8,128)(2,1)S(1)}, bf16[528,1280]{1,0:T(8,128)(2,1)}, u32[]{:S(2)}, u32[]{:S(2)}) collective-permute-start(bf16[528,1280]{1,0:T(8,128)(2,1)S(1)} %fusion.1), channel_id=1, source_target_pairs={{0,1},{1,0},{2,3},{3,2},{4,5},{5,4},{6,7},{7,6},{8,9},{9,8},{10,11... | collective-permute-start | bytes 4055048 | tf_op jit(solution)/shard_map/ppermute | solution.py:69
  52.1 2.9 collective-permute-done.4
  59.5 4.4 %all-to-all-start.1 = ((bf16[4,144,1280]{2,1,0:T(8,128)(2,1)}), bf16[4,144,1280]{2,1,0:T(8,128)(2,1)S(1)}, u32[]{:S(2)}, u32[]{:S(2)}) async-start(bf16[4,144,1280]{2,1,0:T(8,128)(2,1)} %pad_maximum_fusion.2), calls=%async_computation.1 | async-start | bytes 2949120 | tf_op jit(solution)/shard_map/all_to_all | solution.py:410
  82.0 6.3 %collective-permute-done.5 = bf16[640,256]{1,0:T(8,128)(2,1)S(1)} collective-permute-done((bf16[640,256]{1,0:T(8,128)(2,1)S(1)}, bf16[640,256]{1,0:T(8,128)(2,1)S(1)}, u32[]{:S(2)}, u32[]{:S(2)}) %collective-permute-start.5) | collective-permute-done | bytes 327712 | tf_op jit(solution)/shard_map/ppermute | solution.py:69
  92.7 4.5 %collective-permute-start.17 = (bf16[1280,256]{1,0:T(8,128)(2,1)}, bf16[1280,256]{1,0:T(8,128)(2,1)}, u32[]{:S(2)}, u32[]{:S(2)}) collective-permute-start(bf16[1280,256]{1,0:T(8,128)(2,1)} %pad_maximum_fusion.8), channel_id=1, source_target_pairs={{0,8},{4,12},{1,9},{5,13},{2,10},{6,14},{3,11},{7,15},{16,24},{20,... | collective-permute-start | bytes 1966088 | tf_op jit(solution)/shard_map/ppermute | solution.py:436
  106.9 2.7 collective-permute-start.8
  115.8 6.8 %collective-permute-done.19 = bf16[2,16,5120]{2,1,0:T(8,128)(2,1)S(1)} collective-permute-done((bf16[2,16,5120]{2,1,0:T(8,128)(2,1)S(1)}, bf16[2,16,5120]{2,1,0:T(8,128)(2,1)S(1)}, u32[]{:S(2)}, u32[]{:S(2)}) %collective-permute-start.19) | collective-permute-done | bytes 327712 | tf_op jit(solution)/shard_map/ppermute | solution.py:73
  130.3 6.0 %convolution_convert_fusion.2 = bf16[128,1024]{1,0:T(8,128)(2,1)S(1)} fusion(bf16[128,5120]{1,0:T(8,128)(2,1)} %bitcast.169, bf16[5120,1024]{1,0:T(8,128)(2,1)} %param.24), kind=kOutput, calls=%fused_computation.17 | convolution fusion | flops 1342308352 | bytes 12058624 | tf_op jit(solution)/shard_map/dot_general | solution.py:452
  139.9 9.4 %collective-permute-start.23 = (bf16[3840,256]{1,0:T(8,128)(2,1)S(1)}, bf16[3840,256]{1,0:T(8,128)(2,1)}, u32[]{:S(2)}, u32[]{:S(2)}) collective-permute-start(bf16[3840,256]{1,0:T(8,128)(2,1)S(1)} %pad_maximum_fusion), channel_id=1, source_target_pairs={{0,1},{1,0},{2,3},{3,2},{4,5},{5,4},{6,7},{7,6},{8,9},{9,8},{10,11... | collective-permute-start | bytes 5898248 | tf_op jit(solution)/shard_map/ppermute | solution.py:69
  154.4 4.8 %collective-permute-done.24 = bf16[128,1024]{1,0:T(8,128)(2,1)S(1)} collective-permute-done((bf16[128,1024]{1,0:T(8,128)(2,1)S(1)}, bf16[128,1024]{1,0:T(8,128)(2,1)S(1)}, u32[]{:S(2)}, u32[]{:S(2)}) %collective-permute-start.24) | collective-permute-done | bytes 262176 | tf_op jit(solution)/shard_map/ppermute | solution.py:69
  160.0 2.7 collective-permute-start.26
  163.6 2.7 collective-permute-start.15
  166.4 14.7 %collective-permute-done.14 = bf16[128,1024]{1,0:T(8,128)(2,1)S(1)} collective-permute-done((bf16[128,1024]{1,0:T(8,128)(2,1)S(1)}, bf16[128,1024]{1,0:T(8,128)(2,1)S(1)}, u32[]{:S(2)}, u32[]{:S(2)}) %collective-permute-start.14) | collective-permute-done | bytes 262176 | tf_op jit(solution)/shard_map/ppermute | solution.py:73
  182.4 9.3 %shard_map.163 = (bf16[128,512]{1,0:T(8,128)(2,1)S(1)}, bf16[128,256]{1,0:T(8,128)(2,1)S(1)}) custom-call(s32[8]{0:T(128)S(1)} %fusion.52.order_ref, bf16[8,128,1024]{2,1,0:T(8,128)(2,1)} %copy-done.9, f32[8,1,1024]{2,1,0:T(1,128)S(1)} %bitcast.162, bf16[8192,512]{1,0:T(8,128)(2,1)} %query_weight_ref.3, bf16[2,8192,128]{2,1,0:T(8,128)(2,1)} %kv_weight_ref.3), custom_call_target="tpu_custom_call" | custom-call | flops 1610612736 | bytes 14680064 | tf_op jit(solution)/shard_map/pallas_call | solution.py:296
  192.8 9.2 %all-to-all-start.2 = ((bf16[16,128,256]{2,1,0:T(8,128)(2,1)}), bf16[16,128,256]{2,1,0:T(8,128)(2,1)S(1)}, u32[]{:S(2)}, u32[]{:S(2)}) async-start(bf16[16,128,256]{2,1,0:T(8,128)(2,1)} %broadcast_in_dim.98), calls=%async_computation.2 | async-start | bytes 2097152 | tf_op jit(solution)/shard_map/all_to_all | solution.py:63
  204.0 2.7 collective-permute-start.28
  215.6 9.3 %shard_map.164 = (bf16[128,512]{1,0:T(8,128)(2,1)S(1)}, bf16[128,256]{1,0:T(8,128)(2,1)S(1)}) custom-call(s32[8]{0:T(128)S(1)} %fusion.52.order_ref, bf16[8,128,1024]{2,1,0:T(8,128)(2,1)} %bitcast_dynamic-update-slice_fusion.rows_ref, f32[8,1,1024]{2,1,0:T(1,128)S(1)} %bitcast.163, bf16[8192,512]{1,0:T(8,128)(2,1)} %query_weight_ref.3, ...), custom_call_target="tpu_custom_call" | custom-call | flops 1610612736 | bytes 14680064 | tf_op jit(solution)/shard_map/pallas_call | solution.py:296
  227.0 6.7 %all-to-all-start.3 = ((bf16[16,96,512]{2,1,0:T(8,128)(2,1)}), bf16[16,96,512]{2,1,0:T(8,128)(2,1)S(1)}, u32[]{:S(2)}, u32[]{:S(2)}) async-start(bf16[16,96,512]{2,1,0:T(8,128)(2,1)} %pad_maximum_fusion.1), calls=%async_computation.3 | async-start | bytes 3145728 | tf_op jit(solution)/shard_map/all_to_all | solution.py:513
  243.1 9.8 %all-to-all-done.3.last_ref = bf16[16,96,512]{2,1,0:T(8,128)(2,1)S(1)} async-done(((bf16[16,96,512]{2,1,0:T(8,128)(2,1)}), bf16[16,96,512]{2,1,0:T(8,128)(2,1)S(1)}, u32[]{:S(2)}, u32[]{:S(2)}) %all-to-all-start.3) | async-done | bytes 1572896 | tf_op jit(solution)/shard_map/all_to_all | solution.py:513
  257.4 32.2 %shard_map.165 = bf16[640,512]{1,0:T(8,128)(2,1)} custom-call(s32[4]{0:T(128)S(1)} %copy-done.5, s32[512]{0:T(512)S(1)} %add.313.image_src, s32[512]{0:T(512)S(1)} %get-tuple-element.75.image_dst, s32[512]{0:T(512)S(1)} %get-tuple-element.74.image_len, s32[9]{0:T(128)S(1)} %copy-done.4, bf16[640,512]{1,0:T(8,128)(2,1)S(1)} %copy-done.6, ...), custom_call_target="tpu_custom_call" | custom-call | flops 8000000000 | bytes 8000000 | tf_op jit(solution)/shard_map/pallas_call | solution.py:247
  (253 shorter events, 94.5 us)
Async XLA Ops:
  5.4 11.6 %collective-permute-start = (bf16[128,1280]{1,0:T(8,128)(2,1)S(1)}, bf16[128,1280]{1,0:T(8,128)(2,1)S(1)}, u32[]{:S(2)}, u32[]{:S(2)}) collective-permute-start(bf16[128,1280]{1,0:T(8,128)(2,1)S(1)} %get-tuple-element.42), channel_id=1, source_target_pairs={{0,4},{4,8},{8,12},{12,0},{1,5},{5,9},{9,13},{13,1},{2,6},{6,10},{... | collective-permute-start | bytes 983048 | tf_op jit(solution)/shard_map/ppermute | solution.py:380
  7.0 10.0 %collective-permute-start.1 = (bf16[128,1280]{1,0:T(8,128)(2,1)S(1)}, bf16[128,1280]{1,0:T(8,128)(2,1)S(1)}, u32[]{:S(2)}, u32[]{:S(2)}) collective-permute-start(bf16[128,1280]{1,0:T(8,128)(2,1)S(1)} %get-tuple-element.42), channel_id=1, source_target_pairs={{0,8},{4,12},{8,0},{12,4},{1,9},{5,13},{9,1},{13,5},{2,10},{6,14},... | collective-permute-start | bytes 983048 | tf_op jit(solution)/shard_map/ppermute | solution.py:380
  8.1 16.3 %collective-permute-start.2 = (bf16[128,1280]{1,0:T(8,128)(2,1)S(1)}, bf16[128,1280]{1,0:T(8,128)(2,1)}, u32[]{:S(2)}, u32[]{:S(2)}) collective-permute-start(bf16[128,1280]{1,0:T(8,128)(2,1)S(1)} %get-tuple-element.42), channel_id=1, source_target_pairs={{0,12},{4,0},{8,4},{12,8},{1,13},{5,1},{9,5},{13,9},{2,14},{6,2},{... | collective-permute-start | bytes 983048 | tf_op jit(solution)/shard_map/ppermute | solution.py:380
  10.1 31.7 %all-to-all-start = ((bf16[16,48,1280]{2,1,0:T(8,128)(2,1)}), bf16[16,48,1280]{2,1,0:T(8,128)(2,1)S(1)}, u32[]{:S(2)}, u32[]{:S(2)}) async-start(bf16[16,48,1280]{2,1,0:T(8,128)(2,1)} %broadcast_in_dim.73), calls=%async_computation | async-start | bytes 3932160 | tf_op jit(solution)/shard_map/all_to_all | solution.py:372
  59.5 29.6 %all-to-all-start.1 = ((bf16[4,144,1280]{2,1,0:T(8,128)(2,1)}), bf16[4,144,1280]{2,1,0:T(8,128)(2,1)S(1)}, u32[]{:S(2)}, u32[]{:S(2)}) async-start(bf16[4,144,1280]{2,1,0:T(8,128)(2,1)} %pad_maximum_fusion.2), calls=%async_computation.1 | async-start | bytes 2949120 | tf_op jit(solution)/shard_map/all_to_all | solution.py:410
  79.6 8.7 %collective-permute-start.5 = (bf16[640,256]{1,0:T(8,128)(2,1)S(1)}, bf16[640,256]{1,0:T(8,128)(2,1)S(1)}, u32[]{:S(2)}, u32[]{:S(2)}) collective-permute-start(bf16[640,256]{1,0:T(8,128)(2,1)S(1)} %copy-done.11), channel_id=1, source_target_pairs={{0,2},{2,0},{1,3},{3,1},{4,6},{6,4},{5,7},{7,5},{8,10},{10,8},{9,1... | collective-permute-start | bytes 983048 | tf_op jit(solution)/shard_map/ppermute | solution.py:69
  92.7 31.6 %collective-permute-start.17 = (bf16[1280,256]{1,0:T(8,128)(2,1)}, bf16[1280,256]{1,0:T(8,128)(2,1)}, u32[]{:S(2)}, u32[]{:S(2)}) collective-permute-start(bf16[1280,256]{1,0:T(8,128)(2,1)} %pad_maximum_fusion.8), channel_id=1, source_target_pairs={{0,8},{4,12},{1,9},{5,13},{2,10},{6,14},{3,11},{7,15},{16,24},{20,... | collective-permute-start | bytes 1966088 | tf_op jit(solution)/shard_map/ppermute | solution.py:436
  97.3 28.8 %collective-permute-start.16 = (bf16[1280,256]{1,0:T(8,128)(2,1)}, bf16[1280,256]{1,0:T(8,128)(2,1)}, u32[]{:S(2)}, u32[]{:S(2)}) collective-permute-start(bf16[1280,256]{1,0:T(8,128)(2,1)} %pad_maximum_fusion.8), channel_id=1, source_target_pairs={{0,4},{4,8},{8,12},{1,5},{5,9},{9,13},{2,6},{6,10},{10,14},{3,7},{... | collective-permute-start | bytes 1966088 | tf_op jit(solution)/shard_map/ppermute | solution.py:435
  111.6 11.0 %collective-permute-start.19 = (bf16[2,16,5120]{2,1,0:T(8,128)(2,1)S(1)}, bf16[2,16,5120]{2,1,0:T(8,128)(2,1)S(1)}, u32[]{:S(2)}, u32[]{:S(2)}) collective-permute-start(bf16[2,16,5120]{2,1,0:T(8,128)(2,1)S(1)} %pad_maximum_fusion.13), channel_id=1, source_target_pairs={{0,16},{16,32},{32,48},{48,0},{1,17},{17,33},{33,49},{49,1},{2,18}... | collective-permute-start | bytes 983048 | tf_op jit(solution)/shard_map/ppermute | solution.py:73
  114.0 8.7 %collective-permute-start.20 = (bf16[2,16,5120]{2,1,0:T(8,128)(2,1)S(1)}, bf16[2,16,5120]{2,1,0:T(8,128)(2,1)S(1)}, u32[]{:S(2)}, u32[]{:S(2)}) collective-permute-start(bf16[2,16,5120]{2,1,0:T(8,128)(2,1)S(1)} %pad_maximum_fusion.13), channel_id=1, source_target_pairs={{0,48},{16,0},{32,16},{48,32},{1,49},{17,1},{33,17},{49,33},{2,50}... | collective-permute-start | bytes 983048 | tf_op jit(solution)/shard_map/ppermute | solution.py:73
  115.4 12.3 %collective-permute-start.9 = (bf16[16,5120]{1,0:T(8,128)(2,1)S(1)}, bf16[16,5120]{1,0:T(8,128)(2,1)S(1)}, u32[]{:S(2)}, u32[]{:S(2)}) collective-permute-start(bf16[16,5120]{1,0:T(8,128)(2,1)S(1)} %slice_bitcast_fusion.7), channel_id=1, source_target_pairs={{0,16},{16,32},{32,48},{48,0},{1,17},{17,33},{33,49},{49,1},{2,18}... | collective-permute-start | bytes 491528 | tf_op jit(solution)/shard_map/ppermute | solution.py:73
  124.3 12.0 %collective-permute-start.22 = (bf16[16,5120]{1,0:T(8,128)(2,1)S(1)}, bf16[16,5120]{1,0:T(8,128)(2,1)S(1)}, u32[]{:S(2)}, u32[]{:S(2)}) collective-permute-start(bf16[16,5120]{1,0:T(8,128)(2,1)S(1)} %slice_bitcast_fusion.4), channel_id=1, source_target_pairs={{0,48},{16,0},{32,16},{48,32},{1,49},{17,1},{33,17},{49,33},{2,50}... | collective-permute-start | bytes 491528 | tf_op jit(solution)/shard_map/ppermute | solution.py:73
  138.3 13.3 %collective-permute-start.11 = (bf16[128,1024]{1,0:T(8,128)(2,1)S(1)}, bf16[128,1024]{1,0:T(8,128)(2,1)S(1)}, u32[]{:S(2)}, u32[]{:S(2)}) collective-permute-start(bf16[128,1024]{1,0:T(8,128)(2,1)S(1)} %constant_dynamic-update-slice_fusion.9), channel_id=1, source_target_pairs={{0,64},{64,0},{1,65},{65,1},{2,66},{66,2},{3,67},{67,3},{4,68},{68... | collective-permute-start | bytes 786440 | tf_op jit(solution)/shard_map/ppermute | solution.py:69
  139.9 73.4 %collective-permute-start.23 = (bf16[3840,256]{1,0:T(8,128)(2,1)S(1)}, bf16[3840,256]{1,0:T(8,128)(2,1)}, u32[]{:S(2)}, u32[]{:S(2)}) collective-permute-start(bf16[3840,256]{1,0:T(8,128)(2,1)S(1)} %pad_maximum_fusion), channel_id=1, source_target_pairs={{0,1},{1,0},{2,3},{3,2},{4,5},{5,4},{6,7},{7,6},{8,9},{9,8},{10,11... | collective-permute-start | bytes 5898248 | tf_op jit(solution)/shard_map/ppermute | solution.py:69
  149.2 9.9 %collective-permute-start.24 = (bf16[128,1024]{1,0:T(8,128)(2,1)S(1)}, bf16[128,1024]{1,0:T(8,128)(2,1)S(1)}, u32[]{:S(2)}, u32[]{:S(2)}) collective-permute-start(bf16[128,1024]{1,0:T(8,128)(2,1)S(1)} %constant_dynamic-update-slice_fusion.25), channel_id=1, source_target_pairs={{0,64},{64,0},{1,65},{65,1},{2,66},{66,2},{3,67},{67,3},{4,68},{68... | collective-permute-start | bytes 786440 | tf_op jit(solution)/shard_map/ppermute | solution.py:69
  151.6 11.8 %collective-permute-start.12 = (bf16[2,128,1024]{2,1,0:T(8,128)(2,1)S(1)}, bf16[2,128,1024]{2,1,0:T(8,128)(2,1)S(1)}, u32[]{:S(2)}, u32[]{:S(2)}) collective-permute-start(bf16[2,128,1024]{2,1,0:T(8,128)(2,1)S(1)} %pad_maximum_fusion.9), channel_id=1, source_target_pairs={{0,16},{16,32},{32,48},{48,0},{1,17},{17,33},{33,49},{49,1},{2,18}... | collective-permute-start | bytes 1572872 | tf_op jit(solution)/shard_map/ppermute | solution.py:73
  151.7 11.8 %collective-permute-start.13 = (bf16[2,128,1024]{2,1,0:T(8,128)(2,1)S(1)}, bf16[2,128,1024]{2,1,0:T(8,128)(2,1)S(1)}, u32[]{:S(2)}, u32[]{:S(2)}) collective-permute-start(bf16[2,128,1024]{2,1,0:T(8,128)(2,1)S(1)} %pad_maximum_fusion.9), channel_id=1, source_target_pairs={{0,48},{16,0},{32,16},{48,32},{1,49},{17,1},{33,17},{49,33},{2,50}... | collective-permute-start | bytes 1572872 | tf_op jit(solution)/shard_map/ppermute | solution.py:73
  160.0 42.0 %collective-permute-start.25 = (bf16[2,128,1024]{2,1,0:T(8,128)(2,1)}, bf16[2,128,1024]{2,1,0:T(8,128)(2,1)}, u32[]{:S(2)}, u32[]{:S(2)}) collective-permute-start(bf16[2,128,1024]{2,1,0:T(8,128)(2,1)} %pad_maximum_fusion.10), channel_id=1, source_target_pairs={{0,16},{16,32},{32,48},{48,0},{1,17},{17,33},{33,49},{49,1},{2,18}... | collective-permute-start | bytes 1572872 | tf_op jit(solution)/shard_map/ppermute | solution.py:73
  160.0 43.1 %collective-permute-start.26 = (bf16[2,128,1024]{2,1,0:T(8,128)(2,1)}, bf16[2,128,1024]{2,1,0:T(8,128)(2,1)}, u32[]{:S(2)}, u32[]{:S(2)}) collective-permute-start(bf16[2,128,1024]{2,1,0:T(8,128)(2,1)} %pad_maximum_fusion.10), channel_id=1, source_target_pairs={{0,48},{16,0},{32,16},{48,32},{1,49},{17,1},{33,17},{49,33},{2,50}... | collective-permute-start | bytes 1572872 | tf_op jit(solution)/shard_map/ppermute | solution.py:73
  163.5 17.6 %collective-permute-start.14 = (bf16[128,1024]{1,0:T(8,128)(2,1)S(1)}, bf16[128,1024]{1,0:T(8,128)(2,1)S(1)}, u32[]{:S(2)}, u32[]{:S(2)}) collective-permute-start(bf16[128,1024]{1,0:T(8,128)(2,1)S(1)} %slice_bitcast_fusion.3), channel_id=1, source_target_pairs={{0,16},{16,32},{32,48},{48,0},{1,17},{17,33},{33,49},{49,1},{2,18}... | collective-permute-start | bytes 786440 | tf_op jit(solution)/shard_map/ppermute | solution.py:73
  163.6 17.5 %collective-permute-start.15 = (bf16[128,1024]{1,0:T(8,128)(2,1)S(1)}, bf16[128,1024]{1,0:T(8,128)(2,1)S(1)}, u32[]{:S(2)}, u32[]{:S(2)}) collective-permute-start(bf16[128,1024]{1,0:T(8,128)(2,1)S(1)} %slice_bitcast_fusion.2), channel_id=1, source_target_pairs={{0,48},{16,0},{32,16},{48,32},{1,49},{17,1},{33,17},{49,33},{2,50}... | collective-permute-start | bytes 786440 | tf_op jit(solution)/shard_map/ppermute | solution.py:73
  192.8 22.8 %all-to-all-start.2 = ((bf16[16,128,256]{2,1,0:T(8,128)(2,1)}), bf16[16,128,256]{2,1,0:T(8,128)(2,1)S(1)}, u32[]{:S(2)}, u32[]{:S(2)}) async-start(bf16[16,128,256]{2,1,0:T(8,128)(2,1)} %broadcast_in_dim.98), calls=%async_computation.2 | async-start | bytes 2097152 | tf_op jit(solution)/shard_map/all_to_all | solution.py:63
  203.0 8.8 %collective-permute-start.27 = (bf16[128,1024]{1,0:T(8,128)(2,1)S(1)}, bf16[128,1024]{1,0:T(8,128)(2,1)S(1)}, u32[]{:S(2)}, u32[]{:S(2)}) collective-permute-start(bf16[128,1024]{1,0:T(8,128)(2,1)S(1)} %slice_bitcast_fusion.1), channel_id=1, source_target_pairs={{0,16},{16,32},{32,48},{48,0},{1,17},{17,33},{33,49},{49,1},{2,18}... | collective-permute-start | bytes 786440 | tf_op jit(solution)/shard_map/ppermute | solution.py:73
  227.0 25.9 %all-to-all-start.3 = ((bf16[16,96,512]{2,1,0:T(8,128)(2,1)}), bf16[16,96,512]{2,1,0:T(8,128)(2,1)S(1)}, u32[]{:S(2)}, u32[]{:S(2)}) async-start(bf16[16,96,512]{2,1,0:T(8,128)(2,1)} %pad_maximum_fusion.1), calls=%async_computation.3 | async-start | bytes 3145728 | tf_op jit(solution)/shard_map/all_to_all | solution.py:513
  (35 other events, 214.3 us)
